TPU v7x, 256 devices: a whole 4x4x8 slice. The times are simulated.
256 devices in a mesh: adapter: 32 (over z, x_hi, core), tensor: 8 (over y, x_lo).
Axes of the slice: x: 4 (x_hi: 2, x_lo: 2; x = x_hi * 2 + x_lo), y: 4, z: 8, core: 2. Of those that a mesh axis runs over, the one named last changes fastest.
Arguments:
- acts: bfloat16 [65536, 8192], P(('adapter', 'tensor')), may hold values from -6 to 6
- output_gradient: bfloat16 [65536, 1024], P(('adapter', 'tensor')), may hold values from -6 to 6
- adapter_middle_saved: bfloat16 [65536, 16], P(('adapter', 'tensor')), may hold values from -4 to 4
- adapter_per_row: int32 [65536], P(('adapter', 'tensor')), may hold values from 0 to 128, as said below
- segment_first_row: int32 [32, 13], P('adapter'), may hold values from 0 to 1920, as said below
- adapter_per_slot: int32 [32, 13], replicated, may hold values from 0 to 127, as said below
- adapter_storage_row: int32 [128], replicated, may hold values from 0 to 127, as said below
- frozen_value_weight: bfloat16 [8192, 1024], P('tensor'), may hold values from -0.1875 to 0.1875
- slot_down_matrix: bfloat16 [32, 13, 16, 8192], P('adapter', None, None, 'tensor'), may hold values from -1.5 to 1.5
- slot_up_matrix: bfloat16 [32, 13, 16, 1024], P('adapter'), may hold values from -0.1875 to 0.1875
- down_matrix_rows: float32 [128, 16, 8192], P('adapter', None, 'tensor'), may hold values from -1.5 to 1.5
- down_first_moment: float32 [128, 16, 8192], P('adapter', None, 'tensor'), may hold values from -12 to 12
- down_second_moment: float32 [128, 16, 8192], P('adapter', None, 'tensor'), may hold values from 1 to 100
- up_matrix_rows: float32 [128, 16, 1024], P('adapter', None, 'tensor'), may hold values from -0.1875 to 0.1875
- up_first_moment: float32 [128, 16, 1024], P('adapter', None, 'tensor'), may hold values from -12 to 12
- up_second_moment: float32 [128, 16, 1024], P('adapter', None, 'tensor'), may hold values from 1 to 100
Outputs:
- in_grad: bfloat16 [65536, 8192], P(('adapter', 'tensor'))
- new_down: float32 [128, 16, 8192], P('adapter', None, 'tensor')
- new_down_m: float32 [128, 16, 8192], P('adapter', None, 'tensor')
- new_down_v: float32 [128, 16, 8192], P('adapter', None, 'tensor')
- new_up: float32 [128, 16, 1024], P('adapter', None, 'tensor')
- new_up_m: float32 [128, 16, 1024], P('adapter', None, 'tensor')
- new_up_v: float32 [128, 16, 1024], P('adapter', None, 'tensor')
Inputs may be any that keep to these rules, and one draw needn't show every extreme that they name: `adapter_storage_row`: a permutation. `adapter_per_slot`: the 13 adapters of a group are distinct; of one group's slots at most 2 have adapters whose storage row lies on one device (rows d * 4 to d * 4 + 3), and exactly 2 do for some device in every group. `segment_first_row`: each row of a group starts at 0, rises strictly, holds multiples of 128, and ends at 1920; slot k's segment runs to the next offset or to the group's end. `adapter_per_row`: within slot k's segment of group g the rows carry adapter_per_slot[g, k], followed by 1 to 127 padding rows that carry 128.
All inputs are finite; a program needn't handle non-finite values.
Results may differ from a plain program's by a relative error of at most 0.0054.
Values may be sent and summed in bfloat16 or wider, within the bound.
A program may use at most 128 MiB of HBM per device.

v0:
```python
import jax
import jax.numpy as jnp
from jax import lax
from jax.sharding import PartitionSpec as P

TILE = 128
CAP = 2
STEP = 100


adapter_scale = 0.5
beta_one = 0.9
beta_two = 0.999
adam_eps = 1e-08
learn_rate = 0.01


def adam_update(param, first, second, grad):
    first_new = beta_one * first + (1.0 - beta_one) * grad
    second_new = beta_two * second + (1.0 - beta_two) * grad * grad
    bias_one = 1.0 - beta_one**STEP
    bias_two = 1.0 - beta_two**STEP
    moved = first_new / bias_one / (jnp.sqrt(second_new / bias_two) + adam_eps)
    return (param - learn_rate * moved, first_new, second_new)


def body(
    acts,
    output_gradient,
    adapter_middle_saved,
    adapter_per_row,
    segment_first_row,
    adapter_per_slot,
    adapter_storage_row,
    frozen_value_weight,
    slot_down_matrix,
    slot_up_matrix,
    down_matrix_rows,
    down_first_moment,
    down_second_moment,
    up_matrix_rows,
    up_first_moment,
    up_second_moment,
):
    groups = lax.axis_size("adapter")
    shards = lax.axis_size("tensor")
    group_id = lax.axis_index("adapter")
    shard_id = lax.axis_index("tensor")
    local_rows = acts.shape[0]
    rows_of_group = local_rows * shards
    tiles = rows_of_group // TILE
    adapter_list = adapter_storage_row.shape[0]
    slot_count = adapter_per_slot.shape[1]
    rank_dim = slot_up_matrix.shape[2]
    width = frozen_value_weight.shape[1]
    stored_rows = down_matrix_rows.shape[0]
    my_slots = lax.dynamic_index_in_dim(adapter_per_slot, group_id, 0, keepdims=False)
    group_member = adapter_per_row[:, None] == my_slots[None, :]
    up_flat = slot_up_matrix[0].reshape(slot_count * rank_dim, width)
    projected_rows = lax.dot_general(
        output_gradient, up_flat, (((1,), (1,)), ((), ())), preferred_element_type=jnp.float32
    )
    projected_rows = projected_rows.reshape(local_rows, slot_count, rank_dim)
    backward_middle = (
        adapter_scale * jnp.sum(jnp.where(group_member[:, :, None], projected_rows, 0.0), axis=1)
    ).astype(jnp.bfloat16)
    retained_middle = jnp.where(
        (adapter_per_row < adapter_list)[:, None],
        adapter_middle_saved,
        jnp.zeros_like(adapter_middle_saved),
    )
    full_grad, full_back, full_mid = (
        lax.all_gather(output_gradient, "tensor", axis=0, tiled=True),
        lax.all_gather(backward_middle, "tensor", axis=0, tiled=True),
        lax.all_gather(retained_middle, "tensor", axis=0, tiled=True),
    )
    starts = jnp.arange(tiles, dtype=jnp.int32) * TILE
    offsets = segment_first_row[0]
    tile_slot = jnp.sum((offsets[None, :] <= starts[:, None]).astype(jnp.int32), axis=1) - 1
    slot_lookup_table = (
        tile_slot[None, :] == jnp.arange(slot_count, dtype=jnp.int32)[:, None]
    ).astype(jnp.float32)
    frozen_share = lax.dot_general(
        full_grad, frozen_value_weight, (((1,), (1,)), ((), ())), preferred_element_type=jnp.float32
    )
    down_blocks = jnp.take(slot_down_matrix[0], tile_slot, axis=0)
    backward_blocks = full_back.reshape(tiles, TILE, rank_dim)
    adapter_share = jnp.einsum(
        "ahw,awu->ahu", backward_blocks, down_blocks, preferred_element_type=jnp.float32
    )
    input_share = (frozen_share + adapter_share.reshape(rows_of_group, -1)).astype(jnp.bfloat16)
    in_grad = lax.all_to_all(input_share, "tensor", split_axis=0, concat_axis=1, tiled=True)
    column_width = width // shards
    grad_cols = lax.dynamic_slice_in_dim(full_grad, shard_id * column_width, column_width, 1)
    up_fragments = jnp.einsum(
        "tkr,tkc->trc",
        full_mid.reshape(tiles, TILE, rank_dim),
        grad_cols.reshape(tiles, TILE, column_width),
        preferred_element_type=jnp.float32,
    )
    up_gradient = adapter_scale * jnp.einsum(
        "qz,zli->qli", slot_lookup_table, up_fragments, precision=lax.Precision.HIGHEST
    )
    spread = jnp.where(
        group_member[:, :, None], backward_middle[:, None, :], jnp.zeros((), jnp.bfloat16)
    )
    spread = spread.reshape(local_rows, slot_count * rank_dim)
    summed = lax.psum_scatter(
        lax.dot_general(
            acts, spread, (((0,), (0,)), ((), ())), preferred_element_type=jnp.float32
        ).astype(jnp.bfloat16),
        "tensor",
        scatter_dimension=0,
        tiled=True,
    ).astype(jnp.float32)
    down_grad = summed.reshape(-1, slot_count, rank_dim).transpose(1, 2, 0)
    lookup = (
        adapter_per_slot[:, :, None] == jnp.arange(adapter_list, dtype=jnp.int32)[None, None, :]
    )
    stored = jnp.sum(jnp.where(lookup, adapter_storage_row[None, None, :], 0), axis=2)
    owner = stored // stored_rows
    local_row = stored % stored_rows
    earlier = jnp.arange(slot_count)[None, :] < jnp.arange(slot_count)[:, None]
    rank_in = jnp.sum(
        ((owner[:, :, None] == owner[:, None, :]) & earlier[None, :, :]).astype(jnp.int32), axis=2
    )
    my_owner = lax.dynamic_index_in_dim(owner, group_id, 0, keepdims=False)
    my_rank = lax.dynamic_index_in_dim(rank_in, group_id, 0, keepdims=False)
    bucket = jnp.arange(groups * CAP, dtype=jnp.int32)
    packing = ((my_owner * CAP + my_rank)[None, :] == bucket[:, None]).astype(jnp.float32)
    send_down = jnp.einsum(
        "pk,krd->prd", packing, down_grad, precision=lax.Precision.HIGHEST
    ).reshape(groups, CAP, rank_dim, -1)
    send_up = jnp.einsum(
        "pk,krc->prc", packing, up_gradient, precision=lax.Precision.HIGHEST
    ).reshape(groups, CAP, rank_dim, -1)
    got_down, got_up = (
        lax.all_to_all(
            send_down.astype(jnp.bfloat16), "adapter", split_axis=0, concat_axis=0, tiled=True
        ).astype(send_down.dtype),
        lax.all_to_all(
            send_up.astype(jnp.bfloat16), "adapter", split_axis=0, concat_axis=0, tiled=True
        ).astype(send_up.dtype),
    )
    hits = owner == group_id
    cap_index = jnp.arange(CAP, dtype=jnp.int32)
    row_index = jnp.arange(stored_rows, dtype=jnp.int32)
    landing = (
        hits[None, :, :, None]
        & (rank_in[None, :, :, None] == cap_index[None, None, None, :])
        & (local_row[None, :, :, None] == row_index[:, None, None, None])
    )
    receive_table = jnp.sum(landing.astype(jnp.float32), axis=2).reshape(stored_rows, groups * CAP)
    grad_down = jnp.einsum(
        "jp,prd->jrd",
        receive_table,
        got_down.reshape(groups * CAP, rank_dim, -1),
        precision=lax.Precision.HIGHEST,
    )
    grad_up = jnp.einsum(
        "jp,prc->jrc",
        receive_table,
        got_up.reshape(groups * CAP, rank_dim, -1),
        precision=lax.Precision.HIGHEST,
    )
    new_down, new_down_m, new_down_v = adam_update(
        down_matrix_rows, down_first_moment, down_second_moment, grad_down
    )
    new_up, new_up_m, new_up_v = adam_update(
        up_matrix_rows, up_first_moment, up_second_moment, grad_up
    )
    return (in_grad, new_down, new_down_m, new_down_v, new_up, new_up_m, new_up_v)


def solution(mesh):
    in_specs = (
        P(("adapter", "tensor"), None),
        P(("adapter", "tensor"), None),
        P(("adapter", "tensor"), None),
        P(("adapter", "tensor")),
        P("adapter", None),
        P(),
        P(),
        P("tensor", None),
        P("adapter", None, None, "tensor"),
        P("adapter", None, None, None),
        P("adapter", None, "tensor"),
        P("adapter", None, "tensor"),
        P("adapter", None, "tensor"),
        P("adapter", None, "tensor"),
        P("adapter", None, "tensor"),
        P("adapter", None, "tensor"),
    )
    out_specs = (
        P(("adapter", "tensor"), None),
        P("adapter", None, "tensor"),
        P("adapter", None, "tensor"),
        P("adapter", None, "tensor"),
        P("adapter", None, "tensor"),
        P("adapter", None, "tensor"),
        P("adapter", None, "tensor"),
    )
    return jax.shard_map(body, mesh=mesh, in_specs=in_specs, out_specs=out_specs, check_vma=False)
```

profile of v0, /device:TPU:1, one launch (start us, length us, event | category | flops | bytes accessed | tf_op | source)
XLA Modules:
  0.0 329.4 jit_solution(1565534823915908046)
XLA Ops:
  7.2 0.0 copy-start
  7.2 0.0 all-gather.2.cloned.1.call-start
  7.2 0.7 all-gather.2.cloned.1.call-update
  7.9 0.0 reduce-scatter.2.cloned.1.call-start
  8.0 0.9 dynamic-slice_reduce_fusion
  8.9 0.8 broadcast_compare_fusion
  9.6 1.5 fusion.7
  11.2 0.0 copy-start.9
  11.2 0.0 copy-start.12
  11.2 0.0 copy-start.11
  11.2 0.0 copy-start.10
  11.2 0.0 copy-start.13
  11.2 5.0 %fusion = bf16[8192,208]{0,1:T(8,128)(2,1)} fusion(bf16[256,208]{0,1:T(8,128)(2,1)S(1)} %bitcast.77, bf16[256,8192]{1,0:T(8,128)(2,1)} %param.16), kind=kOutput, calls=%fused_computation.2 | convolution fusion | flops 874119168 | bytes 7708672 | tf_op jit(solution)/shard_map/dot_general | solution.py:109
  16.2 0.0 reduce-scatter.2.cloned.1.call-update
  16.3 0.0 copy-done.9
  16.3 0.4 select_reduce_fusion
  16.7 0.1 convert_reduce_fusion
  16.9 0.2 add_reduce_fusion
  17.1 25.3 %all_gather.11 = bf16[2048,16]{0,1:T(8,128)(2,1)S(1)} all-gather(bf16[256,16]{0,1:T(8,128)(2,1)S(1)} %broadcast_select_fusion.1), channel_id=1, replica_groups=mesh['adapter'=32,'tensor'=8] {'tensor'}, dimensions={0}, use_global_device_ids=true | all-gather | bytes 73728 | tf_op jit(solution)/shard_map/all_gather | solution.py:75
  42.4 0.2 convert_reduce_fusion.2
  42.6 65.1 %all-gather.2.cloned.1.call-done = bf16[2048,1024]{1,0:T(8,128)(2,1)} async-done(((bf16[256,1024]{1,0:T(8,128)(2,1)}), bf16[2048,1024]{1,0:T(8,128)(2,1)}) %all-gather.2.cloned.1.call-update) | async-done | bytes 4194320 | tf_op jit(solution)/shard_map/all_gather | solution.py:73
  107.6 1.1 constant_dynamic-slice_fusion
  108.7 0.2 fusion.19
  109.0 0.2 convolution_multiply_fusion
  109.2 0.5 convolution_convert_fusion.2
  109.7 0.9 copy.153
  110.6 10.3 %all-to-all-start.2 = ((bf16[32,2,16,128]{3,1,2,0:T(2,128)(2,1)}), bf16[32,2,16,128]{3,1,2,0:T(2,128)(2,1)S(1)}, u32[]{:S(2)}, u32[]{:S(2)}) async-start(bf16[32,2,16,128]{3,1,2,0:T(2,128)(2,1)} %copy.153), calls=%async_computation.3 | async-start | bytes 524288 | tf_op jit(solution)/shard_map/all_to_all | solution.py:141
  120.9 71.4 %reduce-scatter.2.cloned.1.call-done = bf16[1024,208]{0,1:T(8,128)(2,1)} async-done(((bf16[8192,208]{0,1:T(8,128)(2,1)}), bf16[1024,208]{0,1:T(8,128)(2,1)}) %reduce-scatter.2.cloned.1.call-update) | async-done | bytes 426000 | tf_op jit(solution)/shard_map/reduce_scatter | solution.py:108
  192.2 3.1 convolution_convert_fusion.1
  195.4 4.1 %convert_element_type.50 = bf16[32,2,16,1024]{3,1,0,2:T(2,128)(2,1)} reshape(bf16[64,16,1024]{2,0,1:T(8,128)(2,1)} %convolution_convert_fusion.1) | data formatting | bytes 4194304 | tf_op jit(solution)/shard_map/convert_element_type | solution.py:139
  199.5 5.2 %copy.146 = bf16[32,2,16,1024]{3,1,2,0:T(2,128)(2,1)} copy(bf16[32,2,16,1024]{3,1,0,2:T(2,128)(2,1)} %convert_element_type.50) | data formatting | bytes 4194304 | tf_op jit(solution)/shard_map/convert_element_type | solution.py:139
  204.7 0.0 all-to-all-done.2
  204.7 9.1 %all-to-all-start.1 = ((bf16[32,2,16,1024]{3,1,2,0:T(2,128)(2,1)}), bf16[32,2,16,1024]{3,1,2,0:T(2,128)(2,1)}, u32[]{:S(2)}, u32[]{:S(2)}) async-start(bf16[32,2,16,1024]{3,1,2,0:T(2,128)(2,1)} %copy.146), calls=%async_computation.2 | async-start | bytes 4194304 | tf_op jit(solution)/shard_map/all_to_all | solution.py:138
  213.8 0.6 gather_fusion
  214.4 25.8 %all_gather.10 = bf16[2048,16]{0,1:T(8,128)(2,1)S(1)} all-gather(bf16[256,16]{0,1:T(8,128)(2,1)S(1)} %multiply_convert_fusion), channel_id=1, replica_groups=mesh['adapter'=32,'tensor'=8] {'tensor'}, dimensions={0}, use_global_device_ids=true | all-gather | bytes 73728 | tf_op jit(solution)/shard_map/all_gather | solution.py:74
  240.2 1.3 fusion.11
  241.6 0.9 copy-done.5
  242.4 6.9 %fusion.1 = bf16[2048,1024]{1,0:T(8,128)(2,1)} fusion(f32[16,128,1024]{2,1,0:T(8,128)S(1)} %fusion.11, bf16[2048,1024]{1,0:T(8,128)(2,1)S(1)} %copy-done.5, bf16[1024,1024]{1,0:T(8,128)(2,1)S(1)} %copy-done), kind=kOutput, calls=%fused_computation.4 | convolution fusion | flops 4299161600 | bytes 18874368 | tf_op jit(solution)/shard_map/dot_general | solution.py:83
  249.3 14.7 %all-to-all-done.1 = bf16[32,2,16,1024]{3,1,2,0:T(2,128)(2,1)} async-done(((bf16[32,2,16,1024]{3,1,2,0:T(2,128)(2,1)}), bf16[32,2,16,1024]{3,1,2,0:T(2,128)(2,1)}, u32[]{:S(2)}, u32[]{:S(2)}) %all-to-all-start.1) | async-done | bytes 2097184 | tf_op jit(solution)/shard_map/all_to_all | solution.py:138
  263.9 0.0 copy-start.3
  264.0 0.0 copy-start.4
  264.0 4.9 %all-to-all-start = ((bf16[8,256,1024]{2,1,0:T(8,128)(2,1)}), bf16[8,256,1024]{2,1,0:T(8,128)(2,1)}, u32[]{:S(2)}, u32[]{:S(2)}) async-start(bf16[8,256,1024]{2,1,0:T(8,128)(2,1)} %bitcast.71), calls=%async_computation | async-start | bytes 8388608 | tf_op jit(solution)/shard_map/all_to_all | solution.py:92
  268.9 0.3 convolution_bitcast_fusion
  269.3 0.7 multiply_subtract_fusion.1
  269.9 3.5 %fusion.4 = f32[4,16,1024]{2,0,1:T(4,128)S(1)} fusion(bf16[32,2,16,1024]{3,1,2,0:T(2,128)(2,1)} %all-to-all-done.1, f32[4,32,2]{1,0,2:T(4,128)S(1)} %convert_reduce_fusion.1), kind=kOutput, calls=%fused_computation.9 | convolution fusion | flops 50331648 | bytes 2360320 | tf_op jit(solution)/shard_map/jp,prd->jrd/dot_general | solution.py:154
  273.4 1.1 multiply_subtract_fusion
  274.5 43.2 %all-to-all-done = bf16[8,256,1024]{2,1,0:T(8,128)(2,1)} async-done(((bf16[8,256,1024]{2,1,0:T(8,128)(2,1)}), bf16[8,256,1024]{2,1,0:T(8,128)(2,1)}, u32[]{:S(2)}, u32[]{:S(2)}) %all-to-all-start) | async-done | bytes 4194336 | tf_op jit(solution)/shard_map/all_to_all | solution.py:92
  317.7 4.8 %copy.162 = bf16[8,32,8,1024]{3,2,0,1:T(8,128)(2,1)} copy(bf16[8,32,8,1024]{3,2,1,0:T(8,128)(2,1)} %bitcast.27) | data formatting | bytes 8388608 | tf_op jit(solution)/shard_map/all_to_all | solution.py:92
  (33 shorter events, 0.2 us)
Async XLA Ops:
  7.2 234.4 %copy-start = (bf16[1024,1024]{1,0:T(8,128)(2,1)S(1)}, bf16[1024,1024]{1,0:T(8,128)(2,1)}, u32[]{:S(2)}) copy-start(bf16[1024,1024]{1,0:T(8,128)(2,1)} %param.23) | copy-start | bytes 6291460
  7.2 100.5 %all-gather.2.cloned.1.call-start = ((), (), s32[]{:S(2)}) async-start(), calls=%async_computation.4 | async-start | bytes 4718592 | tf_op jit(solution)/shard_map/all_gather | solution.py:73
  7.9 184.3 %reduce-scatter.2.cloned.1.call-start = ((), (), s32[]{:S(2)}) async-start(), calls=%async_computation.5 | async-start | bytes 3833856 | tf_op jit(solution)/shard_map/reduce_scatter | solution.py:108
  11.2 5.1 %copy-start.9 = (s32[32,13]{0,1:T(8,128)S(1)}, s32[32,13]{0,1:T(8,128)}, u32[]{:S(2)}) copy-start(s32[32,13]{0,1:T(8,128)} %param.21) | copy-start | bytes 4996
  11.2 5.1 %copy-start.12 = (s32[128]{0:T(128)S(1)}, s32[128]{0:T(128)}, u32[]{:S(2)}) copy-start(s32[128]{0:T(128)} %param.22) | copy-start | bytes 1540
  11.2 5.9 %copy-start.11 = (s32[256]{0:T(256)S(1)}, s32[256]{0:T(256)}, u32[]{:S(2)}) copy-start(s32[256]{0:T(256)} %param.19) | copy-start | bytes 3076
  11.2 5.9 %copy-start.10 = (bf16[256,16]{0,1:T(8,128)(2,1)S(1)}, bf16[256,16]{0,1:T(8,128)(2,1)}, u32[]{:S(2)}) copy-start(bf16[256,16]{0,1:T(8,128)(2,1)} %param.18) | copy-start | bytes 24580
  11.2 31.2 %copy-start.13 = (s32[1,13]{1,0:T(1,128)S(1)}, s32[1,13]{1,0:T(1,128)}, u32[]{:S(2)}) copy-start(s32[1,13]{1,0:T(1,128)} %param.20) | copy-start | bytes 160
  110.6 94.1 %all-to-all-start.2 = ((bf16[32,2,16,128]{3,1,2,0:T(2,128)(2,1)}), bf16[32,2,16,128]{3,1,2,0:T(2,128)(2,1)S(1)}, u32[]{:S(2)}, u32[]{:S(2)}) async-start(bf16[32,2,16,128]{3,1,2,0:T(2,128)(2,1)} %copy.153), calls=%async_computation.3 | async-start | bytes 524288 | tf_op jit(solution)/shard_map/all_to_all | solution.py:141
  199.5 14.3 %copy-start.1 = (bf16[1,13,16,1024]{3,2,1,0:T(8,128)(2,1)S(1)}, bf16[1,13,16,1024]{3,2,1,0:T(8,128)(2,1)}, u32[]{:S(2)}) copy-start(bf16[1,13,16,1024]{3,2,1,0:T(8,128)(2,1)} %param.24) | copy-start | bytes 1277956
  204.7 59.3 %all-to-all-start.1 = ((bf16[32,2,16,1024]{3,1,2,0:T(2,128)(2,1)}), bf16[32,2,16,1024]{3,1,2,0:T(2,128)(2,1)}, u32[]{:S(2)}, u32[]{:S(2)}) async-start(bf16[32,2,16,1024]{3,1,2,0:T(2,128)(2,1)} %copy.146), calls=%async_computation.2 | async-start | bytes 4194304 | tf_op jit(solution)/shard_map/all_to_all | solution.py:138
  240.2 2.2 copy-start.5
  263.9 5.3 %copy-start.6 = (f32[4,16,128]{2,1,0:T(8,128)S(1)}, f32[4,16,128]{2,1,0:T(8,128)}, u32[]{:S(2)}) copy-start(f32[4,16,128]{2,1,0:T(8,128)} %param.29) | copy-start | bytes 98308
  263.9 5.3 %copy-start.7 = (f32[4,16,128]{2,1,0:T(8,128)S(1)}, f32[4,16,128]{2,1,0:T(8,128)}, u32[]{:S(2)}) copy-start(f32[4,16,128]{2,1,0:T(8,128)} %param.30) | copy-start | bytes 98308
  263.9 5.3 %copy-start.8 = (f32[4,16,128]{2,1,0:T(8,128)S(1)}, f32[4,16,128]{2,1,0:T(8,128)}, u32[]{:S(2)}) copy-start(f32[4,16,128]{2,1,0:T(8,128)} %param.31) | copy-start | bytes 98308
  263.9 9.4 %copy-start.2 = (f32[4,16,1024]{2,1,0:T(8,128)S(1)}, f32[4,16,1024]{2,1,0:T(8,128)}, u32[]{:S(2)}) copy-start(f32[4,16,1024]{2,1,0:T(8,128)} %param.26) | copy-start | bytes 786436
  263.9 9.4 %copy-start.3 = (f32[4,16,1024]{2,1,0:T(8,128)S(1)}, f32[4,16,1024]{2,1,0:T(8,128)}, u32[]{:S(2)}) copy-start(f32[4,16,1024]{2,1,0:T(8,128)} %param.27) | copy-start | bytes 786436
  264.0 9.4 %copy-start.4 = (f32[4,16,1024]{2,1,0:T(8,128)S(1)}, f32[4,16,1024]{2,1,0:T(8,128)}, u32[]{:S(2)}) copy-start(f32[4,16,1024]{2,1,0:T(8,128)} %param.28) | copy-start | bytes 786436
  264.0 53.8 %all-to-all-start = ((bf16[8,256,1024]{2,1,0:T(8,128)(2,1)}), bf16[8,256,1024]{2,1,0:T(8,128)(2,1)}, u32[]{:S(2)}, u32[]{:S(2)}) async-start(bf16[8,256,1024]{2,1,0:T(8,128)(2,1)} %bitcast.71), calls=%async_computation | async-start | bytes 8388608 | tf_op jit(solution)/shard_map/all_to_all | solution.py:92
Sparse Core Ops, SparseCore 0:
  9.8 97.7 all-gather.1
  110.8 81.4 reduce-scatter.1
where the time goes:
time: 330 us; the launch traced here: 329 us
  waiting for transfers between devices  195 us (59%)
  blocking collectives  51.1 us (15%)
  starting transfers between devices  24.4 us (7%)
  matrix products  22.5 us (7%)
  local copies, waits for them, and re-layouts  18.5 us (6%)
  between operations  14.4 us (4%)
  other arithmetic  3.59 us (1%)
    reduce_scatter x1, waiting for transfers between devices, body(): lax.psum_scatter(lax.dot_general(acts, spread, (((0,), (0,)), ((), ())),...  71.4 us
    all_gather x1, waiting for transfers between devices, body(): lax.all_gather(output_gradient, 'tensor', axis=0, tiled=True)  65.1 us
    all_to_all x1, waiting for transfers between devices, body(): lax.all_to_all(input_share, 'tensor', split_axis=0, concat_axis=1, tiled=...  43.2 us
    all_gather x1, blocking collectives, body(): lax.all_gather(backward_middle, 'tensor', axis=0, tiled=True)  25.8 us
    all_gather x1, blocking collectives, body(): lax.all_gather(retained_middle, 'tensor', axis=0, tiled=True)  25.3 us
    all_to_all x1, waiting for transfers between devices, body(): lax.all_to_all(send_down.astype(jnp.bfloat16), 'adapter', split_axis=0, c...  14.7 us
    all_to_all x1, starting transfers between devices, body(): lax.all_to_all(send_up.astype(jnp.bfloat16), 'adapter', split_axis=0, con...  10.3 us
    convert_element_type x2, local copies, waits for them, and re-layouts, body(): send_down.astype(jnp.bfloat16)  9.28 us
  transfers between devices with their start and end apart: 5, of which 4 were waited for; matrix products, arithmetic and copies ran while one was open for 12% of the time, Pallas kernels for 0%

commit v1 on v0

v1 whole, which is shorter than its diff:
```python
import jax
import jax.numpy as jnp
from jax import lax
from jax.experimental import pallas as pl
from jax.experimental.pallas import tpu as pltpu
from jax.sharding import PartitionSpec as P

MESH = pl.DeviceIdType.MESH
TILE = 128
STEP = 100
NX, NY, NZ = 4, 4, 8

adapter_scale = 0.5
beta_one = 0.9
beta_two = 0.999
adam_eps = 1e-08
learn_rate = 0.01

ROWS = 256
WIDTH = 8192
KVW = 1024
RANK = 16
SLOTS = 13
TILES = 16
COLS = 1024
UPC = 128
PAY = COLS + UPC
CHUNK = 128
STORED = 4
A, B, C, X, AX, BX, DX = range(7)
F32 = jnp.float32
BF16 = jnp.bfloat16


def adam_update(param, first, second, grad):
    first_new = beta_one * first + (1.0 - beta_one) * grad
    second_new = beta_two * second + (1.0 - beta_two) * grad * grad
    bias_one = 1.0 - beta_one**STEP
    bias_two = 1.0 - beta_two**STEP
    moved = first_new / bias_one / (jnp.sqrt(second_new / bias_two) + adam_eps)
    return (param - learn_rate * moved, first_new, second_new)


def kernel(
    acts_h, og_h, mid, rid, seg, aps, stor, w_h, sd_h, su_h,
    out_h, gd, gu,
    acts, og, sd, su, w, xd, dn, gs, gr, sl, dns, us, ur, ds, dr, bmt, ost,
    tslot, sr, tab,
    in_sem, out_sem, w_send, w_recv, sib_recv, dn_send, dn_recv, g_send, g_recv,
    s_send, s_recv, r_send, r_recv, loc_sem,
):
    a = lax.axis_index("adapter")
    t = lax.axis_index("tensor")
    z, xh, c = a // 4, (a // 2) % 2, a % 2
    y, xl = t // 2, t % 2
    x = xh * 2 + xl

    def dev(dx=0, dy=0, dz=0, dc=0):
        x_, y_, z_, c_ = (x + dx) % NX, (y + dy) % NY, (z + dz) % NZ, (c + dc) % 2
        return (z_ * 4 + (x_ // 2) * 2 + c_, y_ * 2 + x_ % 2)

    def peer(dy, dx):
        return (a, ((y + dy) % NY) * 2 + (xl + dx) % 2)

    loads = {}
    for i, (name, src, dst) in enumerate(
        (
            ("og", og_h, og),
            ("su", su_h, su),
            ("sd", sd_h, sd),
            ("acts", acts_h, acts),
            ("w", w_h, w.at[t]),
        )
    ):
        loads[name] = pltpu.make_async_copy(src, dst, in_sem.at[i])
        loads[name].start()

    barrier = pltpu.get_barrier_semaphore()
    friends = [peer(dy, dx) for dy in range(4) for dx in range(2) if (dy, dx) != (0, 0)]
    other = 1 - 2 * (1 - xl)
    friends += [dev(dx=other), dev(dx=2), dev(dz=1), dev(dz=-1), dev(dc=1)]
    for f in friends:
        pl.semaphore_signal(barrier, inc=1, device_id=f, device_id_type=MESH)

    def tile_slot(j, _):
        n = jnp.int32(-1)
        for k in range(SLOTS):
            n = n + (seg[0, k] <= j * TILE).astype(jnp.int32)
        tslot[j] = n
        return 0

    lax.fori_loop(0, TILES, tile_slot, 0)

    loads["og"].wait()
    loads["su"].wait()
    kept = []
    for i in range(2):
        slot = tslot[2 * t + i]
        ids = rid[:, i * TILE : (i + 1) * TILE]
        prod = lax.dot_general(
            su[slot], og[i * TILE : (i + 1) * TILE], (((1,), (1,)), ((), ())), preferred_element_type=F32
        )
        bmt[i] = jnp.where(ids == aps[a, slot], adapter_scale * prod, 0.0).astype(BF16)
        m = mid[i * TILE : (i + 1) * TILE].astype(F32).T
        kept.append(jnp.where(ids < stor.shape[0], m, 0.0).astype(BF16))

    pl.semaphore_wait(barrier, len(friends))

    e = z % 2
    p0, p1 = 2 * e, 2 * e + 1
    n0, n1 = 2 * (1 - e), 2 * (1 - e) + 1
    where = {
        A: ((y + 1) % 4) * 2 + xl,
        B: ((y + 3) % 4) * 2 + xl,
        C: ((y + 2) % 4) * 2 + xl,
        X: y * 2 + 1 - xl,
        AX: ((y + 1) % 4) * 2 + 1 - xl,
        BX: ((y + 3) % 4) * 2 + 1 - xl,
        DX: ((y + 2) % 4) * 2 + 1 - xl,
    }
    sent = []

    def region(piece, chunk, half):
        return w.at[piece, pl.ds(pl.multiple_of(half * 512 + chunk * CHUNK, CHUNK), CHUNK)]

    def push(src, dst, sem, target):
        cp = pltpu.make_async_remote_copy(
            src_ref=src, dst_ref=dst, send_sem=w_send.at[len(sent)], recv_sem=sem, device_id=target, device_id_type=MESH
        )
        cp.start()
        sent.append(cp)

    def push_own(chunk, label, target):
        src = w_h.at[pl.ds(pl.multiple_of(c * 512 + chunk * CHUNK, CHUNK), CHUNK)]
        push(src, region(t, chunk, c), w_recv.at[label, chunk], target)

    def pass_on(label, chunk, new, target):
        place = region(where[label], chunk, c)
        push(place, place, w_recv.at[new, chunk], target)

    def arrived(label, chunk):
        place = region(where[label], chunk, c)
        pltpu.make_async_copy(place, place, w_recv.at[label, chunk]).wait()
        push(place, place, sib_recv.at[label, chunk], dev(dc=1))

    def sib_arrived(label):
        for chunk in range(4):
            place = region(where[label], chunk, 1 - c)
            pltpu.make_async_copy(place, place, sib_recv.at[label, chunk]).wait()

    up_y, dn_y, up_x, dn_x, up_z, dn_z = dev(dy=1), dev(dy=-1), dev(dx=1), dev(dx=-1), dev(dz=1), dev(dz=-1)

    push_own(p0, B, up_y)
    push_own(p0, A, dn_y)
    push_own(p0, X, up_x)
    push_own(p1, X, dn_x)
    push_own(p1, B, up_y)
    push_own(p1, A, dn_y)

    loads["acts"].wait()
    for i in range(2):
        upg = adapter_scale * jnp.dot(kept[i], og[i * TILE : (i + 1) * TILE], preferred_element_type=F32)
        upg = upg.astype(BF16)
        for u in range(8):
            gs[u, i, :, COLS:] = upg[:, u * UPC : (u + 1) * UPC]
    order = [(2, 1), (2, 0), (1, 1), (3, 1), (0, 1), (1, 0), (3, 0), (0, 0)]
    g_sent = []
    for n, (dy, dx) in enumerate(order):
        u = ((y + dy) % 4) * 2 + (xl + dx) % 2
        for i in range(2):
            block = acts[i * TILE : (i + 1) * TILE, pl.ds(pl.multiple_of(u * COLS, COLS), COLS)]
            gs[u, i, :, :COLS] = jnp.dot(bmt[i], block, preferred_element_type=F32).astype(BF16)
        if (dy, dx) == (0, 0):
            gr[t] = gs[t]
        else:
            cp = pltpu.make_async_remote_copy(
                src_ref=gs.at[u], dst_ref=gr.at[t], send_sem=g_send.at[n], recv_sem=g_recv.at[n],
                device_id=peer(dy, dx), device_id_type=MESH,
            )
            cp.start()
            g_sent.append(cp)

    loads["sd"].wait()

    def spread(j, _):
        xd[j] = sd[tslot[j]]
        return 0

    lax.fori_loop(0, TILES, spread, 0)
    dn_sent = []
    for n, (dy, dx) in enumerate(order):
        u = ((y + dy) % 4) * 2 + (xl + dx) % 2
        if (dy, dx) == (0, 0):
            dn[t] = xd[pl.ds(2 * t, 2)]
        else:
            cp = pltpu.make_async_remote_copy(
                src_ref=xd.at[pl.ds(2 * u, 2)], dst_ref=dn.at[t], send_sem=dn_send.at[n], recv_sem=dn_recv.at[n],
                device_id=peer(dy, dx), device_id_type=MESH,
            )
            cp.start()
            dn_sent.append(cp)

    def in_grad(piece, n):
        def block(j, _):
            rows = pl.ds(pl.multiple_of(j * 256, 256), 256)
            cols = pl.ds(pl.multiple_of(piece * COLS + j * 256, 256), 256)
            full = lax.dot_general(og[...], w[piece, rows], (((1,), (1,)), ((), ())), preferred_element_type=F32)
            for i in range(2):
                low = lax.dot_general(
                    bmt[i], dn[piece, i, :, rows], (((0,), (0,)), ((), ())), preferred_element_type=F32
                )
                ost[i * TILE : (i + 1) * TILE, cols] = (full[i * TILE : (i + 1) * TILE] + low).astype(BF16)
            return 0

        lax.fori_loop(0, 4, block, 0)
        cols = pl.ds(pl.multiple_of(piece * COLS, COLS), COLS)
        cp = pltpu.make_async_copy(ost.at[:, cols], out_h.at[:, cols], out_sem.at[n])
        cp.start()
        return cp

    arrived(A, p0)
    pass_on(A, p0, AX, up_x)
    pass_on(A, p0, C, dn_y)
    arrived(B, p0)
    pass_on(B, p0, BX, dn_x)
    arrived(X, p0)
    pass_on(X, p0, X, up_z)
    arrived(X, p1)
    pass_on(X, p1, X, dn_z)
    arrived(A, p1)
    pass_on(A, p1, AX, dn_x)
    arrived(B, p1)
    pass_on(B, p1, BX, up_x)
    pass_on(B, p1, C, up_y)
    push_own(n0, B, up_y)
    push_own(n0, A, dn_y)
    push_own(n1, B, up_y)
    push_own(n1, A, dn_y)

    outs = []
    loads["w"].wait()
    outs.append(in_grad(t, 0))

    for q in range(4):
        group = z * 4 + (xh ^ (q % 2)) * 2 + (c ^ (q // 2))
        for k in range(SLOTS):
            sr[q * SLOTS + k] = stor[aps[group, k]]

    def find(n, _):
        q, rest = n // 32, n % 32
        row = ((z + rest // 4) % NZ) * 16 + xh * 8 + c * 4 + rest % 4
        k_found = jnp.int32(0)
        for k in range(SLOTS):
            k_found = jnp.where(sr[q * SLOTS + k] == row, k + 1, k_found)
        tab[n] = k_found
        return 0

    lax.fori_loop(0, 128, find, 0)

    for n, (dy, dx) in enumerate(order[:-1]):
        src = ((y + dy) % 4) * 2 + (xl + dx) % 2
        back = order.index(((4 - dy) % 4, dx))
        pltpu.make_async_copy(gr.at[src], gr.at[src], g_recv.at[back]).wait()
    for k in range(SLOTS):
        first = seg[0, k] // TILE
        last = seg[0, k + 1] // TILE if k + 1 < SLOTS else TILES
        total = jnp.zeros((RANK, PAY), F32)
        for i in range(4):
            j = jnp.minimum(first + i, TILES - 1)
            total = total + jnp.where(first + i < last, gr[j // 2, j % 2].astype(F32), 0.0)
        sl[0, k] = total.astype(BF16)
    s_sent = []

    def send_slots(n, src, dst, target):
        cp = pltpu.make_async_remote_copy(
            src_ref=sl.at[src], dst_ref=sl.at[dst], send_sem=s_send.at[n], recv_sem=s_recv.at[dst - 1],
            device_id=target, device_id_type=MESH,
        )
        cp.start()
        s_sent.append(cp)

    send_slots(0, 0, 1, dev(dx=2))
    send_slots(1, 0, 2, dev(dc=1))

    arrived(AX, p0)
    pass_on(AX, p0, AX, up_z)
    arrived(BX, p0)
    pass_on(BX, p0, BX, dn_z)
    arrived(C, p0)
    pass_on(C, p0, DX, up_x)
    arrived(C, p1)
    pass_on(C, p1, DX, dn_x)
    arrived(AX, p1)
    pass_on(AX, p1, AX, dn_z)
    arrived(BX, p1)
    pass_on(BX, p1, BX, up_z)
    pass_on(C, p0, C, up_z)
    pass_on(C, p1, C, dn_z)

    pltpu.make_async_copy(sl.at[1], sl.at[1], s_recv.at[0]).wait()
    send_slots(2, 1, 3, dev(dc=1))
    pltpu.make_async_copy(sl.at[2], sl.at[2], s_recv.at[1]).wait()
    pltpu.make_async_copy(sl.at[3], sl.at[3], s_recv.at[2]).wait()

    def gather_rows(dz):
        def one(r, _):
            total = jnp.zeros((RANK, PAY), F32)
            for q in range(4):
                k = tab[q * 32 + dz * 4 + r]
                total = total + jnp.where(k > 0, sl[q, jnp.maximum(k - 1, 0)].astype(F32), 0.0)
            dns[dz, r] = total
            return 0

        lax.fori_loop(0, STORED, one, 0)

    r_sent = []

    def ring_send(src, dst, direction, step, target):
        n = direction * 4 + step
        cp = pltpu.make_async_remote_copy(
            src_ref=src, dst_ref=dst, send_sem=r_send.at[n], recv_sem=r_recv.at[n], device_id=target, device_id_type=MESH
        )
        cp.start()
        r_sent.append(cp)

    def ring_wait(ref, direction, step):
        pltpu.make_async_copy(ref, ref, r_recv.at[direction * 4 + step]).wait()

    gather_rows(4)
    us[0, 0:2] = dns[4, 0:2].astype(BF16)
    ds[0, 2:4] = dns[4, 2:4].astype(BF16)
    ring_send(us.at[0, pl.ds(0, 2)], ur.at[0, pl.ds(0, 2)], 0, 0, up_z)
    ring_send(ds.at[0, pl.ds(2, 2)], dr.at[0, pl.ds(2, 2)], 1, 0, dn_z)
    gather_rows(3)
    gather_rows(5)
    ring_wait(ur.at[0, pl.ds(0, 2)], 0, 0)
    us[1, 0:2] = (dns[3, 0:2] + ur[0, 0:2].astype(F32)).astype(BF16)
    us[1, 2:4] = dns[3, 2:4].astype(BF16)
    ring_send(us.at[1], ur.at[1], 0, 1, up_z)
    ring_wait(dr.at[0, pl.ds(2, 2)], 1, 0)
    ds[1, 0:2] = dns[5, 0:2].astype(BF16)
    ds[1, 2:4] = (dns[5, 2:4] + dr[0, 2:4].astype(F32)).astype(BF16)
    ring_send(ds.at[1], dr.at[1], 1, 1, dn_z)
    for dz in (2, 6, 1, 7, 0):
        gather_rows(dz)
    arrived(DX, p0)
    pass_on(DX, p0, DX, up_z)
    arrived(DX, p1)
    pass_on(DX, p1, DX, dn_z)
    for step in (2, 3):
        ring_wait(ur.at[step - 1], 0, step - 1)
        us[step] = (dns[4 - step] + ur[step - 1].astype(F32)).astype(BF16)
        ring_send(us.at[step], ur.at[step], 0, step, up_z)
        ring_wait(dr.at[step - 1], 1, step - 1)
        ds[step] = (dns[4 + step] + dr[step - 1].astype(F32)).astype(BF16)
        ring_send(ds.at[step], dr.at[step], 1, step, dn_z)
        if step == 2:
            for n, (dy, dx) in enumerate(order[:-1]):
                src = ((y + dy) % 4) * 2 + (xl + dx) % 2
                back = order.index(((4 - dy) % 4, dx))
                pltpu.make_async_copy(dn.at[src], dn.at[src], dn_recv.at[back]).wait()
            for label in (A, B):
                arrived(label, n0)
                arrived(label, n1)
            for label in (X, AX, BX):
                arrived(label, n0)
                arrived(label, n1)
            for n, label in enumerate((A, B)):
                sib_arrived(label)
                outs.append(in_grad(where[label], 1 + n))
    arrived(C, n0)
    arrived(C, n1)
    arrived(DX, n0)
    arrived(DX, n1)
    for n, label in enumerate((X, AX, BX)):
        sib_arrived(label)
        outs.append(in_grad(where[label], 3 + n))
    ring_wait(ur.at[3], 0, 3)
    ring_wait(dr.at[3], 1, 3)
    total = dns[0] + ur[3].astype(F32) + dr[3].astype(F32)
    gd[...] = total[:, :, :COLS]
    gu[...] = total[:, :, COLS:]
    for n, label in enumerate((C, DX)):
        sib_arrived(label)
        outs.append(in_grad(where[label], 6 + n))

    for cp in sent + g_sent + dn_sent + s_sent + r_sent:
        cp.wait_send()
    for cp in outs:
        cp.wait()


def body(
    acts, output_gradient, adapter_middle_saved, adapter_per_row, segment_first_row, adapter_per_slot,
    adapter_storage_row, frozen_value_weight, slot_down_matrix, slot_up_matrix, down_matrix_rows,
    down_first_moment, down_second_moment, up_matrix_rows, up_first_moment, up_second_moment,
):
    vmem = pl.BlockSpec(memory_space=pltpu.VMEM)
    smem = pl.BlockSpec(memory_space=pltpu.SMEM)
    hbm = pl.BlockSpec(memory_space=pl.ANY)
    dma = pltpu.SemaphoreType.DMA
    in_grad, grad_down, grad_up = pl.pallas_call(
        kernel,
        out_shape=(
            jax.ShapeDtypeStruct((ROWS, WIDTH), BF16),
            jax.ShapeDtypeStruct((STORED, RANK, COLS), F32),
            jax.ShapeDtypeStruct((STORED, RANK, UPC), F32),
        ),
        in_specs=[hbm, hbm, vmem, vmem, smem, smem, smem, hbm, hbm, hbm],
        out_specs=(hbm, vmem, vmem),
        scratch_shapes=[
            pltpu.VMEM((ROWS, WIDTH), BF16),
            pltpu.VMEM((ROWS, KVW), BF16),
            pltpu.VMEM((SLOTS, RANK, COLS), BF16),
            pltpu.VMEM((SLOTS, RANK, KVW), BF16),
            pltpu.VMEM((8, COLS, KVW), BF16),
            pltpu.VMEM((TILES, RANK, COLS), BF16),
            pltpu.VMEM((8, 2, RANK, COLS), BF16),
            pltpu.VMEM((8, 2, RANK, PAY), BF16),
            pltpu.VMEM((8, 2, RANK, PAY), BF16),
            pltpu.VMEM((4, SLOTS, RANK, PAY), BF16),
            pltpu.VMEM((NZ, STORED, RANK, PAY), F32),
            pltpu.VMEM((4, STORED, RANK, PAY), BF16),
            pltpu.VMEM((4, STORED, RANK, PAY), BF16),
            pltpu.VMEM((4, STORED, RANK, PAY), BF16),
            pltpu.VMEM((4, STORED, RANK, PAY), BF16),
            pltpu.VMEM((2, RANK, TILE), BF16),
            pltpu.VMEM((ROWS, WIDTH), BF16),
            pltpu.SMEM((TILES,), jnp.int32),
            pltpu.SMEM((4 * SLOTS,), jnp.int32),
            pltpu.SMEM((128,), jnp.int32),
            dma((5,)),
            dma((8,)),
            dma((64,)),
            dma((7, 4)),
            dma((7, 4)),
            dma((7,)),
            dma((7,)),
            dma((7,)),
            dma((7,)),
            dma((3,)),
            dma((3,)),
            dma((8,)),
            dma((8,)),
            dma((1,)),
        ],
        compiler_params=pltpu.CompilerParams(collective_id=0, has_side_effects=True, vmem_limit_bytes=56 << 20),
        cost_estimate=pl.CostEstimate(flops=2 * ROWS * WIDTH * KVW, bytes_accessed=12 << 20, transcendentals=0),
        name="fused",
    )(
        acts, output_gradient, adapter_middle_saved, adapter_per_row.reshape(1, ROWS), segment_first_row,
        adapter_per_slot, adapter_storage_row, frozen_value_weight, slot_down_matrix[0], slot_up_matrix[0],
    )
    new_down, new_down_m, new_down_v = adam_update(down_matrix_rows, down_first_moment, down_second_moment, grad_down)
    new_up, new_up_m, new_up_v = adam_update(up_matrix_rows, up_first_moment, up_second_moment, grad_up)
    return (in_grad, new_down, new_down_m, new_down_v, new_up, new_up_m, new_up_v)


def solution(mesh):
    rows = ("adapter", "tensor")
    stored = P("adapter", None, "tensor")
    in_specs = (
        P(rows, None), P(rows, None), P(rows, None), P(rows), P("adapter", None), P(), P(), P("tensor", None),
        P("adapter", None, None, "tensor"), P("adapter", None, None, None),
        stored, stored, stored, stored, stored, stored,
    )
    out_specs = (P(rows, None),) + (stored,) * 6
    return jax.shard_map(body, mesh=mesh, in_specs=in_specs, out_specs=out_specs, check_vma=False)
```

time: 330 us -> 96 us (0.29)
  waiting for transfers between devices: 195 us -> 0 us
  Pallas kernels: 0 us -> 84.2 us
  blocking collectives: 51.1 us -> 0 us
  starting transfers between devices: 24.4 us -> 0 us
  matrix products: 22.5 us -> 0 us
  between operations: 14.4 us -> 0.69 us
  local copies, waits for them, and re-layouts: 18.5 us -> 7.47 us
    pallas_call x0 -> x1, Pallas kernels: none -> 84.2 us  [body(): pl.pallas_call(kernel, out_shape=(jax.ShapeDtypeStruct((ROWS, WIDTH), BF1...]
    reduce_scatter x1 -> x0, waiting for transfers between devices: 71.4 us -> none  [body(): lax.psum_scatter(lax.dot_general(acts, spread, (((0,), (0,)), ((), ())),...]
    all_gather x1 -> x0, waiting for transfers between devices: 65.1 us -> none  [body(): lax.all_gather(output_gradient, 'tensor', axis=0, tiled=True)]
    all_to_all x3 -> x0, waiting for transfers between devices: 57.9 us -> none  [the longest x1 43.2 us: body(): lax.all_to_all(input_share, 'tensor', split_axis=0, concat_axis=1, tiled=...]
    all_gather x2 -> x0, blocking collectives: 51.1 us -> none  [the longest x1 25.8 us: body(): lax.all_gather(backward_middle, 'tensor', axis=0, tiled=True)]
    all_to_all x3 -> x0, starting transfers between devices: 24.3 us -> none  [the longest x1 10.3 us: body(): lax.all_to_all(send_up.astype(jnp.bfloat16), 'adapter', split_axis=0, con...]
    dot_general x10 -> x0, matrix products: 22.5 us -> none  [the longest x1 6.86 us: body(): lax.dot_general(full_grad, frozen_value_weight, (((1,), (1,)), ((), ())),...]
    convert_element_type x3 -> x0, local copies, waits for them, and re-layouts: 10.2 us -> none  [the longest x2 9.28 us: body(): send_down.astype(jnp.bfloat16)]
  transfers between devices with their start and end apart: 5 -> 0, of which waited for: 4 -> 0; matrix products, arithmetic and copies ran while one was open for 12% -> 0% of each run, Pallas kernels for 0% -> 0%
where the time goes in v1:
time: 96 us; the launch traced here: 95.7 us
  Pallas kernels  84.2 us (88%)
  local copies, waits for them, and re-layouts  7.47 us (8%)
  other arithmetic  3.34 us (3%)
    pallas_call x1, Pallas kernels, body(): pl.pallas_call(kernel, out_shape=(jax.ShapeDtypeStruct((ROWS, WIDTH), BF1...  84.2 us
    unnamed x15, local copies, waits for them, and re-layouts  7.47 us
    sub x2, other arithmetic, adam_update(): return (param - learn_rate * moved, first_new, second_new)  3.34 us

profile of v1, /device:TPU:1, one launch (start us, length us, event | category | flops | bytes accessed | tf_op | source)
XLA Modules:
  0.0 95.7 jit_solution(1355542127178945634)
XLA Ops:
  0.6 1.4 %copy.24.aps = s32[32,13]{1,0:T(8,128)} copy(s32[32,13]{0,1:T(8,128)} %param.21) | data formatting | bytes 3328 | tf_op args[5]
  2.0 1.4 %copy.23.mid = bf16[256,16]{1,0:T(8,128)(2,1)} copy(bf16[256,16]{0,1:T(8,128)(2,1)} %param.18) | data formatting | bytes 16384 | tf_op args[2]
  3.4 0.0 copy-start.3
  3.4 0.0 copy-start.4
  3.4 0.0 copy-start.5
  3.4 0.0 copy-start
  3.5 0.0 copy-start.1
  3.5 0.0 copy-start.2
  3.5 84.2 %fused.1 = (bf16[256,8192]{1,0:T(8,128)(2,1)}, f32[4,16,1024]{2,1,0:T(8,128)}, f32[4,16,128]{2,1,0:T(8,128)}) custom-call(bf16[256,8192]{1,0:T(8,128)(2,1)} %acts_h.1, bf16[256,1024]{1,0:T(8,128)(2,1)} %og_h.1, bf16[256,16]{1,0:T(8,128)(2,1)} %copy.23.mid, s32[1,256]{1,0:T(1,128)} %bitcast.5, s32[1,13]{1,0:T(1,128)} %seg.1, s32[32,13]{1,0:T(8,128)} %copy.24.aps, ...), custom_call_target="tpu_custom_call" | custom-call | flops 4294967296 | bytes 12582912 | tf_op jit(solution)/shard_map/fused/pallas_call | solution.py:402
  87.7 0.0 copy-done.3
  87.7 0.0 copy-done.4
  87.7 0.0 copy-done.5
  87.7 1.4 %multiply_subtract_fusion.1 = (f32[4,16,128]{2,1,0:T(8,128)}, f32[4,16,128]{2,1,0:T(8,128)}, f32[4,16,128]{2,1,0:T(8,128)}) fusion(f32[4,16,128]{2,1,0:T(8,128)S(1)} %copy-done.3, f32[4,16,128]{2,1,0:T(8,128)} %get-tuple-element.12, f32[4,16,128]{2,1,0:T(8,128)S(1)} %copy-done.4, f32[4,16,128]{2,1,0:T(8,128)S(1)} %copy-done.5), kind=kLoop, calls=%fused_computation.6 | loop fusion | flops 106496 | bytes 229376 | tf_op jit(solution)/shard_map/sub | solution.py:41
  89.1 0.0 copy-done
  89.1 0.0 copy-done.1
  89.1 0.0 copy-done.2
  89.1 1.9 %multiply_subtract_fusion = (f32[4,16,1024]{2,1,0:T(8,128)}, f32[4,16,1024]{2,1,0:T(8,128)}, f32[4,16,1024]{2,1,0:T(8,128)}) fusion(f32[4,16,1024]{2,1,0:T(8,128)S(1)} %copy-done, f32[4,16,1024]{2,1,0:T(8,128)} %get-tuple-element.11, f32[4,16,1024]{2,1,0:T(8,128)S(1)} %copy-done.1, f32[4,16,1024]{2,1,0:T(8,128)S(1)} %copy-done.2), kind=kLoop, calls=%fused_computation.2 | loop fusion | flops 851968 | bytes 1835008 | tf_op jit(solution)/shard_map/sub | solution.py:41
  91.1 4.6 %copy.26 = bf16[256,8192]{1,0:T(8,128)(2,1)} copy(bf16[256,8192]{1,0:T(8,128)(2,1)} %get-tuple-element.26) | data formatting | bytes 8388608
Async XLA Ops:
  3.4 84.2 %copy-start.3 = (f32[4,16,128]{2,1,0:T(8,128)S(1)}, f32[4,16,128]{2,1,0:T(8,128)}, u32[]{:S(2)}) copy-start(f32[4,16,128]{2,1,0:T(8,128)} %param.29) | copy-start | bytes 98308
  3.4 84.3 %copy-start.4 = (f32[4,16,128]{2,1,0:T(8,128)S(1)}, f32[4,16,128]{2,1,0:T(8,128)}, u32[]{:S(2)}) copy-start(f32[4,16,128]{2,1,0:T(8,128)} %param.30) | copy-start | bytes 98308
  3.4 84.3 %copy-start.5 = (f32[4,16,128]{2,1,0:T(8,128)S(1)}, f32[4,16,128]{2,1,0:T(8,128)}, u32[]{:S(2)}) copy-start(f32[4,16,128]{2,1,0:T(8,128)} %param.31) | copy-start | bytes 98308
  3.4 85.7 %copy-start = (f32[4,16,1024]{2,1,0:T(8,128)S(1)}, f32[4,16,1024]{2,1,0:T(8,128)}, u32[]{:S(2)}) copy-start(f32[4,16,1024]{2,1,0:T(8,128)} %param.26) | copy-start | bytes 786436
  3.5 85.7 %copy-start.1 = (f32[4,16,1024]{2,1,0:T(8,128)S(1)}, f32[4,16,1024]{2,1,0:T(8,128)}, u32[]{:S(2)}) copy-start(f32[4,16,1024]{2,1,0:T(8,128)} %param.27) | copy-start | bytes 786436
  3.5 85.7 %copy-start.2 = (f32[4,16,1024]{2,1,0:T(8,128)S(1)}, f32[4,16,1024]{2,1,0:T(8,128)}, u32[]{:S(2)}) copy-start(f32[4,16,1024]{2,1,0:T(8,128)} %param.28) | copy-start | bytes 786436

commit v2 on v1

v2 whole, which is shorter than its diff:
```python
import jax
import jax.numpy as jnp
from jax import lax
from jax.experimental import pallas as pl
from jax.experimental.pallas import tpu as pltpu
from jax.sharding import PartitionSpec as P

MESH = pl.DeviceIdType.MESH
TILE = 128
STEP = 100
NX, NY, NZ = 4, 4, 8

adapter_scale = 0.5
beta_one = 0.9
beta_two = 0.999
adam_eps = 1e-08
learn_rate = 0.01

ROWS = 256
WIDTH = 8192
KVW = 1024
RANK = 16
SLOTS = 13
TILES = 16
COLS = 1024
UPC = 128
PAY = COLS + UPC
CHUNK = 128
STORED = 4
A, B, C, X, AX, BX, DX = range(7)
CUTS = ((0, 640), (640, PAY))
BLOCK = 256
VMEM_LIMIT = 56 << 20
SEQ = (
    ("own_y", 0), ("own_x",), ("own_y", 1),
    ("tiles", 0), ("tiles", 1),
    ("in", A, 0), ("in", B, 0), ("in", X, 0), ("in", X, 1), ("in", A, 1), ("in", B, 1),
    ("tables",), ("slots", 0), ("slots", 1),
    ("in", A, 2), ("in", B, 3), ("in", AX, 0), ("in", BX, 0), ("in", C, 0),
    ("ring", 0, 0), ("ring", 0, 1), ("rest", 0), ("rest", 1),
    ("in", AX, 1), ("in", BX, 1), ("in", C, 1),
    ("ring", 1, 0), ("ring", 1, 1),
    ("downs",),
    ("ring", 2, 0), ("ring", 2, 1),
    ("in", AX, 2), ("in", BX, 3),
    ("ring", 3, 0), ("ring", 3, 1),
    ("cols", None),
    ("in", A, 3), ("in", B, 2), ("in", X, 2), ("in", X, 3),
    ("ring", 4, 0), ("ring", 4, 1),
    ("in", AX, 3), ("in", BX, 2),
    ("in", C, 2), ("in", C, 3), ("in", DX, 0), ("in", DX, 1),
    ("wait_down",), ("cols", A), ("cols", B), ("cols", X), ("cols", AX), ("cols", BX), ("cols", C),
    ("in", DX, 2), ("in", DX, 3), ("cols", DX),
)
F32 = jnp.float32
BF16 = jnp.bfloat16


def adam_update(param, first, second, grad):
    first_new = beta_one * first + (1.0 - beta_one) * grad
    second_new = beta_two * second + (1.0 - beta_two) * grad * grad
    bias_one = 1.0 - beta_one**STEP
    bias_two = 1.0 - beta_two**STEP
    moved = first_new / bias_one / (jnp.sqrt(second_new / bias_two) + adam_eps)
    return (param - learn_rate * moved, first_new, second_new)


def kernel(
    acts_h, og_h, midt, rid, seg, apst, stor, w_h, sd_h, su_h,
    out_h, gd, gu,
    acts, og, sd, su, w, xd, dn,
    gs0, gs1, gr0, gr1, sl0, sl1, dns0, dns1, us0, us1, ur0, ur1, ds0, ds1, dr0, dr1,
    bmt, bm2, ost, tslot, seg2, sr, tab,
    in_sem, out_sem, w_send, w_recv, sib_recv, dn_send, dn_recv, g_send, g_recv,
    s_send, s_recv, r_send, r_recv, m_sem,
):
    gs, gr, sl, dns = (gs0, gs1), (gr0, gr1), (sl0, sl1), (dns0, dns1)
    us, ur, ds, dr = (us0, us1), (ur0, ur1), (ds0, ds1), (dr0, dr1)
    parts = range(len(CUTS))
    a = lax.axis_index("adapter")
    t = lax.axis_index("tensor")
    z, xh, c = a // 4, (a // 2) % 2, a % 2
    y, xl = t // 2, t % 2
    x = xh * 2 + xl

    def dev(dx=0, dy=0, dz=0, dc=0):
        x_, y_, z_, c_ = (x + dx) % NX, (y + dy) % NY, (z + dz) % NZ, (c + dc) % 2
        return (z_ * 4 + (x_ // 2) * 2 + c_, y_ * 2 + x_ % 2)

    def peer(dy, dx, flip=0):
        return (z * 4 + ((xh + flip) % 2) * 2 + c, ((y + dy) % NY) * 2 + (xl + dx) % 2)

    def tensor_of(dy, dx):
        return ((y + dy) % 4) * 2 + (xl + dx) % 2

    loads = {}
    for i, (name, src, dst) in enumerate(
        (
            ("og", og_h, og),
            ("su", su_h, su),
            ("acts", acts_h, acts),
            ("sd", sd_h, sd),
            ("w", w_h, w.at[t]),
        )
    ):
        loads[name] = pltpu.make_async_copy(src, dst, in_sem.at[i])
        loads[name].start()

    plane = [(2, 1), (2, 0), (1, 1), (3, 1), (0, 1), (1, 0), (3, 0), (0, 0)]
    order = [(dy, dx, flip) for dy, dx in plane for flip in (1, 0)]
    barrier = pltpu.get_barrier_semaphore()
    friends = [peer(*d) for d in order[:-1]] + [dev(dz=1), dev(dz=-1), dev(dc=1)]
    for f in friends:
        pl.semaphore_signal(barrier, inc=1, device_id=f, device_id_type=MESH)

    def tile_slot(j, _):
        n = jnp.int32(-1)
        for k in range(SLOTS):
            n = n + (seg[0, k] <= j * TILE).astype(jnp.int32)
        tslot[j] = n
        return 0

    lax.fori_loop(0, TILES, tile_slot, 0)

    loads["og"].wait()
    loads["su"].wait()
    kept = []
    bmt[...] = jnp.zeros_like(bmt)
    for i in range(2):
        slot = tslot[2 * t + i]
        ids = rid[:, i * TILE : (i + 1) * TILE]
        prod = lax.dot_general(
            su[slot], og[i * TILE : (i + 1) * TILE], (((1,), (1,)), ((), ())), preferred_element_type=F32
        )
        own = jnp.where(ids == apst[slot, a], adapter_scale * prod, 0.0)
        bmt[i * RANK : (i + 1) * RANK, i * TILE : (i + 1) * TILE] = own.astype(BF16)
        m = midt[:, i * TILE : (i + 1) * TILE]
        kept.append(jnp.where(ids < stor.shape[0], m, jnp.zeros_like(m)))
    bm2[...] = bmt[...].astype(F32).T.astype(BF16)

    pl.semaphore_wait(barrier, len(friends))

    seg_copy = pltpu.make_async_remote_copy(
        src_ref=seg, dst_ref=seg2, send_sem=m_sem.at[0], recv_sem=m_sem.at[1],
        device_id=peer(0, 0, 1), device_id_type=MESH,
    )
    seg_copy.start()

    e = z % 2
    chunks = (2 * e, 2 * e + 1, 2 * (1 - e), 2 * (1 - e) + 1)
    where = {
        A: tensor_of(1, 0), B: tensor_of(3, 0), C: tensor_of(2, 0), X: tensor_of(0, 1),
        AX: tensor_of(1, 1), BX: tensor_of(3, 1), DX: tensor_of(2, 1),
    }
    sent = []

    def region(piece, chunk, half):
        return w.at[piece, pl.ds(pl.multiple_of(half * 512 + chunk * CHUNK, CHUNK), CHUNK)]

    def push(src, dst, sem, target):
        cp = pltpu.make_async_remote_copy(
            src_ref=src, dst_ref=dst, send_sem=w_send.at[len(sent)], recv_sem=sem, device_id=target, device_id_type=MESH
        )
        cp.start()
        sent.append(cp)

    def push_own(chunk, label, target):
        src = w_h.at[pl.ds(pl.multiple_of(c * 512 + chunk * CHUNK, CHUNK), CHUNK)]
        push(src, region(t, chunk, c), w_recv.at[label, chunk], target)

    def sib_arrived(label):
        for chunk in range(4):
            place = region(where[label], chunk, 1 - c)
            pltpu.make_async_copy(place, place, sib_recv.at[label, chunk]).wait()

    up_y, dn_y, up_x, dn_x, up_z, dn_z = dev(dy=1), dev(dy=-1), dev(dx=1), dev(dx=-1), dev(dz=1), dev(dz=-1)

    def own_y(chunk):
        push_own(chunk, B, up_y)
        push_own(chunk, A, dn_y)

    def own_x():
        push_own(chunks[0], X, up_x)
        push_own(chunks[1], X, dn_x)

    g_sent = []

    def tiles_out(p):
        lo, hi = CUTS[p]
        down = min(hi, COLS) - lo
        if p == 0:
            loads["acts"].wait()
        if hi > COLS:
            for i in range(2):
                g = jnp.dot(kept[i], og[i * TILE : (i + 1) * TILE], preferred_element_type=F32)
                g = (adapter_scale * g).astype(BF16)
                for u in range(8):
                    gs[p][u, i, :, down:] = g[:, u * UPC : (u + 1) * UPC]
        for n, (dy, dx, flip) in enumerate(order):
            u = tensor_of(dy, dx)
            if n % 2 == 0:
                for i in range(2):
                    block = acts[i * TILE : (i + 1) * TILE, pl.ds(pl.multiple_of(u * COLS + lo, 128), down)]
                    low = bmt[i * RANK : (i + 1) * RANK, i * TILE : (i + 1) * TILE]
                    gs[p][u, i, :, :down] = jnp.dot(low, block, preferred_element_type=F32).astype(BF16)
            if n == len(order) - 1:
                gr[p][0, t] = gs[p][t]
            else:
                cp = pltpu.make_async_remote_copy(
                    src_ref=gs[p].at[u], dst_ref=gr[p].at[flip, t], send_sem=g_send.at[p, n], recv_sem=g_recv.at[p, n],
                    device_id=peer(dy, dx, flip), device_id_type=MESH,
                )
                cp.start()
                g_sent.append(cp)

    def wait_tiles(p):
        for dy, dx, flip in order[:-1]:
            back = order.index(((4 - dy) % 4, dx, flip))
            place = gr[p].at[flip, tensor_of(dy, dx)]
            pltpu.make_async_copy(place, place, g_recv.at[p, back]).wait()

    dn_sent = []

    def spread(j, _):
        xd[j // 2, pl.ds(pl.multiple_of((j % 2) * RANK, RANK), RANK)] = sd[tslot[j]]
        return 0

    def downs_out():
        loads["sd"].wait()
        lax.fori_loop(0, TILES, spread, 0)
        for n, (dy, dx) in enumerate(plane):
            u = tensor_of(dy, dx)
            if (dy, dx) == (0, 0):
                dn[t] = xd[t]
            else:
                cp = pltpu.make_async_remote_copy(
                    src_ref=xd.at[u], dst_ref=dn.at[t], send_sem=dn_send.at[n], recv_sem=dn_recv.at[n],
                    device_id=peer(dy, dx), device_id_type=MESH,
                )
                cp.start()
                dn_sent.append(cp)

    def wait_down():
        for dy, dx in plane[:-1]:
            place = dn.at[tensor_of(dy, dx)]
            pltpu.make_async_copy(place, place, dn_recv.at[plane.index(((4 - dy) % 4, dx))]).wait()

    outs = []

    def in_grad(piece):
        for j in range(COLS // BLOCK):
            rows = pl.ds(j * BLOCK, BLOCK)
            cols = pl.ds(pl.multiple_of(piece * COLS + j * BLOCK, BLOCK), BLOCK)
            full = lax.dot_general(og[...], w[piece, rows], (((1,), (1,)), ((), ())), preferred_element_type=F32)
            low = jnp.dot(bm2[...], dn[piece, :, rows], preferred_element_type=F32)
            ost[:, cols] = (full + low).astype(BF16)
        cols = pl.ds(pl.multiple_of(piece * COLS, COLS), COLS)
        cp = pltpu.make_async_copy(ost.at[:, cols], out_h.at[:, cols], out_sem.at[len(outs)])
        cp.start()
        outs.append(cp)

    def find(n, _):
        q, rest = n // 32, n % 32
        row = ((z + rest // 4) % NZ) * 16 + xh * 8 + c * 4 + rest % 4
        k_found = jnp.int32(0)
        for k in range(SLOTS):
            k_found = jnp.where(sr[q * SLOTS + k] == row, k + 1, k_found)
        tab[n] = k_found
        return 0

    def tables():
        for q in range(4):
            group = z * 4 + (xh ^ (q % 2)) * 2 + (c ^ (q // 2))
            for k in range(SLOTS):
                sr[q * SLOTS + k] = stor[apst[k, group]]
        lax.fori_loop(0, 128, find, 0)

    s_sent = []

    def slots_out(p):
        if p == 0:
            seg_copy.wait()
        wait_tiles(p)
        for q, table in ((0, seg), (1, seg2)):
            for k in range(SLOTS):
                first = table[0, k] // TILE
                last = table[0, k + 1] // TILE if k + 1 < SLOTS else TILES
                total = jnp.zeros((RANK, sl[p].shape[-1]), F32)
                for i in range(4):
                    j = jnp.minimum(first + i, TILES - 1)
                    total = total + jnp.where(first + i < last, gr[p][q, j // 2, j % 2].astype(F32), 0.0)
                sl[p][q, k] = total.astype(BF16)
        cp = pltpu.make_async_remote_copy(
            src_ref=sl[p].at[pl.ds(0, 2)], dst_ref=sl[p].at[pl.ds(2, 2)], send_sem=s_send.at[p], recv_sem=s_recv.at[p],
            device_id=dev(dc=1), device_id_type=MESH,
        )
        cp.start()
        s_sent.append(cp)

    def gather_rows(p, dz):
        def one(r, _):
            total = jnp.zeros((RANK, sl[p].shape[-1]), F32)
            for q in range(4):
                k = tab[q * 32 + dz * 4 + r]
                total = total + jnp.where(k > 0, sl[p][q, jnp.maximum(k - 1, 0)].astype(F32), 0.0)
            dns[p][dz, r] = total
            return 0

        lax.fori_loop(0, STORED, one, 0)

    r_sent = []

    def ring_send(src, dst, p, direction, step):
        n = direction * 4 + step
        cp = pltpu.make_async_remote_copy(
            src_ref=src, dst_ref=dst, send_sem=r_send.at[p, n], recv_sem=r_recv.at[p, n],
            device_id=dn_z if direction else up_z, device_id_type=MESH,
        )
        cp.start()
        r_sent.append(cp)

    def ring_wait(ref, p, direction, step):
        pltpu.make_async_copy(ref, ref, r_recv.at[p, direction * 4 + step]).wait()

    def ring(step, p):
        if step == 0:
            place = sl[p].at[pl.ds(2, 2)]
            pltpu.make_async_copy(place, place, s_recv.at[p]).wait()
            gather_rows(p, 4)
            us[p][0, 0:2] = dns[p][4, 0:2].astype(BF16)
            ring_send(us[p].at[0, pl.ds(0, 2)], ur[p].at[0, pl.ds(0, 2)], p, 0, 0)
            ds[p][0, 2:4] = dns[p][4, 2:4].astype(BF16)
            ring_send(ds[p].at[0, pl.ds(2, 2)], dr[p].at[0, pl.ds(2, 2)], p, 1, 0)
            gather_rows(p, 3)
            gather_rows(p, 5)
        elif step == 1:
            ring_wait(ur[p].at[0, pl.ds(0, 2)], p, 0, 0)
            us[p][1, 0:2] = (dns[p][3, 0:2] + ur[p][0, 0:2].astype(F32)).astype(BF16)
            us[p][1, 2:4] = dns[p][3, 2:4].astype(BF16)
            ring_send(us[p].at[1], ur[p].at[1], p, 0, 1)
            ring_wait(dr[p].at[0, pl.ds(2, 2)], p, 1, 0)
            ds[p][1, 0:2] = dns[p][5, 0:2].astype(BF16)
            ds[p][1, 2:4] = (dns[p][5, 2:4] + dr[p][0, 2:4].astype(F32)).astype(BF16)
            ring_send(ds[p].at[1], dr[p].at[1], p, 1, 1)
        elif step < 4:
            ring_wait(ur[p].at[step - 1], p, 0, step - 1)
            us[p][step] = (dns[p][4 - step] + ur[p][step - 1].astype(F32)).astype(BF16)
            ring_send(us[p].at[step], ur[p].at[step], p, 0, step)
            ring_wait(dr[p].at[step - 1], p, 1, step - 1)
            ds[p][step] = (dns[p][4 + step] + dr[p][step - 1].astype(F32)).astype(BF16)
            ring_send(ds[p].at[step], dr[p].at[step], p, 1, step)
        else:
            ring_wait(ur[p].at[3], p, 0, 3)
            ring_wait(dr[p].at[3], p, 1, 3)
            total = dns[p][0] + ur[p][3].astype(F32) + dr[p][3].astype(F32)
            lo, hi = CUTS[p]
            down = min(hi, COLS) - lo
            gd[:, :, lo : lo + down] = total[:, :, :down]
            if hi > COLS:
                gu[...] = total[:, :, down:]

    def gather_rest(p):
        for dz in (2, 6, 1, 7, 0):
            gather_rows(p, dz)

    passing = {
        (A, 0): ((C, dn_y), (AX, up_x), (A, up_z)),
        (A, 1): ((AX, dn_x), (A, dn_z)),
        (A, 2): ((C, dn_y),),
        (B, 0): ((BX, dn_x), (B, dn_z)),
        (B, 1): ((C, up_y), (BX, up_x), (B, up_z)),
        (B, 3): ((C, up_y),),
        (X, 0): ((X, up_z),),
        (X, 1): ((X, dn_z),),
        (AX, 0): ((AX, up_z),),
        (AX, 1): ((AX, dn_z),),
        (BX, 0): ((BX, dn_z),),
        (BX, 1): ((BX, up_z),),
        (C, 0): ((DX, up_x),),
        (C, 1): ((DX, dn_x),),
        (AX, 2): ((DX, dn_y),),
        (BX, 3): ((DX, up_y),),
    }

    def chunk_in(label, n):
        place = region(where[label], chunks[n], c)
        pltpu.make_async_copy(place, place, w_recv.at[label, chunks[n]]).wait()
        for new, target in passing.get((label, n), ()):
            push(place, place, w_recv.at[new, chunks[n]], target)
        push(place, place, sib_recv.at[label, chunks[n]], dev(dc=1))

    def columns(label):
        if label is None:
            loads["w"].wait()
            in_grad(t)
        else:
            sib_arrived(label)
            in_grad(where[label])

    steps = {
        "own_y": lambda n: own_y(chunks[n]),
        "own_x": own_x,
        "tiles": tiles_out,
        "downs": downs_out,
        "tables": tables,
        "slots": slots_out,
        "ring": ring,
        "rest": gather_rest,
        "in": chunk_in,
        "cols": columns,
        "wait_down": wait_down,
    }
    for name, *arg in SEQ:
        steps[name](*arg)

    for cp in sent + g_sent + dn_sent + s_sent + r_sent:
        cp.wait_send()
    for cp in outs:
        cp.wait()


def finish(tmp, *refs):
    ins, outs, bufs, stage, sems = refs[:8], refs[8:15], refs[15:29], refs[29], refs[30]
    step = ROWS // 8
    loads = [pltpu.make_async_copy(ins[i], bufs[i], sems.at[i]) for i in range(8)]
    for i in range(8):
        rows = pl.ds(i * step, step)
        loads.append(pltpu.make_async_copy(tmp.at[rows], stage.at[rows], sems.at[8 + i]))
    for cp in loads:
        cp.start()
    moves = []

    def leave(src, dst):
        cp = pltpu.make_async_copy(src, dst, sems.at[16 + len(moves)])
        cp.start()
        moves.append(cp)

    for cp in loads[:8]:
        cp.wait()
    for half in range(2):
        gr, pr, fi, se = bufs[half * 4 : half * 4 + 4]
        new = adam_update(pr[...], fi[...], se[...], gr[...])
        for i in range(3):
            n = half * 3 + i
            bufs[8 + n][...] = new[i]
            leave(bufs[8 + n], outs[1 + n])
        for i in range(half * 4, half * 4 + 4):
            rows = pl.ds(i * step, step)
            loads[8 + i].wait()
            leave(stage.at[rows], outs[0].at[rows])
    for cp in moves:
        cp.wait()


def body(
    acts, output_gradient, adapter_middle_saved, adapter_per_row, segment_first_row, adapter_per_slot,
    adapter_storage_row, frozen_value_weight, slot_down_matrix, slot_up_matrix, down_matrix_rows,
    down_first_moment, down_second_moment, up_matrix_rows, up_first_moment, up_second_moment,
):
    vmem = pl.BlockSpec(memory_space=pltpu.VMEM)
    smem = pl.BlockSpec(memory_space=pltpu.SMEM)
    hbm = pl.BlockSpec(memory_space=pl.ANY)
    dma = pltpu.SemaphoreType.DMA
    widths = [hi - lo for lo, hi in CUTS]
    n = len(CUTS)

    def each(shape, dtype):
        return [pltpu.VMEM((*shape, width), dtype) for width in widths]

    down_shape, up_shape = (STORED, RANK, COLS), (STORED, RANK, UPC)
    tmp, grad_down, grad_up = pl.pallas_call(
        kernel,
        out_shape=(
            jax.ShapeDtypeStruct((ROWS, WIDTH), BF16),
            jax.ShapeDtypeStruct(down_shape, F32),
            jax.ShapeDtypeStruct(up_shape, F32),
        ),
        in_specs=[hbm, hbm, vmem, vmem, smem, smem, smem, hbm, hbm, hbm],
        out_specs=(hbm, vmem, vmem),
        scratch_shapes=[
            pltpu.VMEM((ROWS, WIDTH), BF16),
            pltpu.VMEM((ROWS, KVW), BF16),
            pltpu.VMEM((SLOTS, RANK, COLS), BF16),
            pltpu.VMEM((SLOTS, RANK, KVW), BF16),
            pltpu.VMEM((8, COLS, KVW), BF16),
            pltpu.VMEM((8, 2 * RANK, COLS), BF16),
            pltpu.VMEM((8, 2 * RANK, COLS), BF16),
            *each((8, 2, RANK), BF16),
            *each((2, 8, 2, RANK), BF16),
            *each((4, SLOTS, RANK), BF16),
            *each((NZ, STORED, RANK), F32),
            *each((4, STORED, RANK), BF16),
            *each((4, STORED, RANK), BF16),
            *each((4, STORED, RANK), BF16),
            *each((4, STORED, RANK), BF16),
            pltpu.VMEM((2 * RANK, ROWS), BF16),
            pltpu.VMEM((ROWS, 2 * RANK), BF16),
            pltpu.VMEM((ROWS, WIDTH), BF16),
            pltpu.SMEM((TILES,), jnp.int32),
            pltpu.SMEM((1, SLOTS), jnp.int32),
            pltpu.SMEM((4 * SLOTS,), jnp.int32),
            pltpu.SMEM((128,), jnp.int32),
            dma((5,)),
            dma((8,)),
            dma((64,)),
            dma((7, 4)),
            dma((7, 4)),
            dma((7,)),
            dma((7,)),
            dma((n, 15)),
            dma((n, 15)),
            dma((n,)),
            dma((n,)),
            dma((n, 8)),
            dma((n, 8)),
            dma((2,)),
        ],
        compiler_params=pltpu.CompilerParams(collective_id=0, has_side_effects=True, vmem_limit_bytes=VMEM_LIMIT),
        cost_estimate=pl.CostEstimate(flops=2 * ROWS * WIDTH * KVW, bytes_accessed=12 << 20, transcendentals=0),
        name="fused",
    )(
        acts, output_gradient, adapter_middle_saved.T, adapter_per_row.reshape(1, ROWS), segment_first_row,
        adapter_per_slot.T, adapter_storage_row, frozen_value_weight, slot_down_matrix[0], slot_up_matrix[0],
    )
    state_down = [jax.ShapeDtypeStruct(down_shape, F32)] * 3
    state_up = [jax.ShapeDtypeStruct(up_shape, F32)] * 3
    return pl.pallas_call(
        finish,
        out_shape=(jax.ShapeDtypeStruct((ROWS, WIDTH), BF16), *state_down, *state_up),
        in_specs=[hbm] * 9,
        out_specs=(hbm,) * 7,
        scratch_shapes=[pltpu.VMEM(down_shape, F32)] * 4
        + [pltpu.VMEM(up_shape, F32)] * 4
        + [pltpu.VMEM(down_shape, F32)] * 3
        + [pltpu.VMEM(up_shape, F32)] * 3
        + [pltpu.VMEM((ROWS, WIDTH), BF16), dma((30,))],
        name="finish",
    )(
        tmp, grad_down, down_matrix_rows, down_first_moment, down_second_moment,
        grad_up, up_matrix_rows, up_first_moment, up_second_moment,
    )


def solution(mesh):
    rows = ("adapter", "tensor")
    stored = P("adapter", None, "tensor")
    in_specs = (
        P(rows, None), P(rows, None), P(rows, None), P(rows), P("adapter", None), P(), P(), P("tensor", None),
        P("adapter", None, None, "tensor"), P("adapter", None, None, None),
        stored, stored, stored, stored, stored, stored,
    )
    out_specs = (P(rows, None),) + (stored,) * 6
    return jax.shard_map(body, mesh=mesh, in_specs=in_specs, out_specs=out_specs, check_vma=False)
```

time: 96 us -> 84.7 us (0.88)
  local copies, waits for them, and re-layouts: 7.47 us -> 0 us
  other arithmetic: 3.34 us -> 0 us
    unnamed x15 -> x0, local copies, waits for them, and re-layouts: 7.47 us -> none
    pallas_call x1, Pallas kernels: 84.2 us -> 79.8 us  [body(): pl.pallas_call(kernel, out_shape=(jax.ShapeDtypeStruct((ROWS, WIDTH), BF1...]
    pallas_call x0 -> x1, Pallas kernels: none -> 4.16 us  [body(): pl.pallas_call(finish, out_shape=(jax.ShapeDtypeStruct((ROWS, WIDTH), BF1...]
    sub x2 -> x0, other arithmetic: 3.34 us -> none  [adam_update(): return (param - learn_rate * moved, first_new, second_new)]
where the time goes in v2:
time: 84.7 us; the launch traced here: 84.6 us
  Pallas kernels  83.9 us (99%)
    pallas_call x1, Pallas kernels, body(): pl.pallas_call(kernel, out_shape=(jax.ShapeDtypeStruct((ROWS, WIDTH), BF1...  79.8 us
    pallas_call x1, Pallas kernels, body(): pl.pallas_call(finish, out_shape=(jax.ShapeDtypeStruct((ROWS, WIDTH), BF1...  4.16 us

profile of v2, /device:TPU:1, one launch (start us, length us, event | category | flops | bytes accessed | tf_op | source)
XLA Modules:
  0.0 84.6 jit_solution(218085892977360411)
XLA Ops:
  0.6 79.8 %fused.1 = (bf16[256,8192]{1,0:T(8,128)(2,1)}, f32[4,16,1024]{2,1,0:T(8,128)}, f32[4,16,128]{2,1,0:T(8,128)}) custom-call(bf16[256,8192]{1,0:T(8,128)(2,1)} %acts_h.1, bf16[256,1024]{1,0:T(8,128)(2,1)} %og_h.1, bf16[16,256]{1,0:T(8,128)(2,1)} %bitcast.7, s32[1,256]{1,0:T(1,128)} %bitcast.9, s32[1,13]{1,0:T(1,128)} %seg.1, s32[13,32]{1,0:T(8,128)} %bitcast.8, ...), custom_call_target="tpu_custom_call" | custom-call | flops 4294967296 | bytes 12582912 | tf_op jit(solution)/shard_map/fused/pallas_call | solution.py:471
  80.4 4.2 %finish.1 = (bf16[256,8192]{1,0:T(8,128)(2,1)}, f32[4,16,1024]{2,1,0:T(8,128)}, f32[4,16,1024]{2,1,0:T(8,128)}, f32[4,16,1024]{2,1,0:T(8,128)}, f32[4,16,128]{2,...) custom-call(bf16[256,8192]{1,0:T(8,128)(2,1)} %get-tuple-element.10.tmp, ...), custom_call_target="tpu_custom_call" | custom-call | tf_op jit(solution)/shard_map/finish/pallas_call | solution.py:527

commit v3 on v2

--- a/solution.py
+++ b/solution.py
@@ -30,27 +30,18 @@
 A, B, C, X, AX, BX, DX = range(7)
 CUTS = ((0, 640), (640, PAY))
 BLOCK = 256
+SUB = 2
 VMEM_LIMIT = 56 << 20
 SEQ = (
-    ("own_y", 0), ("own_x",), ("own_y", 1),
-    ("tiles", 0), ("tiles", 1),
-    ("in", A, 0), ("in", B, 0), ("in", X, 0), ("in", X, 1), ("in", A, 1), ("in", B, 1),
-    ("tables",), ("slots", 0), ("slots", 1),
-    ("in", A, 2), ("in", B, 3), ("in", AX, 0), ("in", BX, 0), ("in", C, 0),
-    ("ring", 0, 0), ("ring", 0, 1), ("rest", 0), ("rest", 1),
-    ("in", AX, 1), ("in", BX, 1), ("in", C, 1),
-    ("ring", 1, 0), ("ring", 1, 1),
-    ("downs",),
-    ("ring", 2, 0), ("ring", 2, 1),
-    ("in", AX, 2), ("in", BX, 3),
-    ("ring", 3, 0), ("ring", 3, 1),
-    ("cols", None),
-    ("in", A, 3), ("in", B, 2), ("in", X, 2), ("in", X, 3),
-    ("ring", 4, 0), ("ring", 4, 1),
-    ("in", AX, 3), ("in", BX, 2),
-    ("in", C, 2), ("in", C, 3), ("in", DX, 0), ("in", DX, 1),
-    ("wait_down",), ("cols", A), ("cols", B), ("cols", X), ("cols", AX), ("cols", BX), ("cols", C),
-    ("in", DX, 2), ("in", DX, 3), ("cols", DX),
+    ("own_y", 0), ("own_y", 1), ("own_x",), ("tables",), ("in", B, 0), ("in", A, 0), ("in", B, 1), ("in", A, 1),
+    ("tiles", 0), ("tiles", 1), ("in", X, 0), ("in", AX, 1), ("in", BX, 1), ("in", X, 1), ("in", AX, 0),
+    ("in", X, 2), ("in", B, 2), ("downs",), ("cols", None), ("in", BX, 0), ("in", C, 1), ("in", AX, 3),
+    ("slots", 0), ("ring", 0, 0), ("rest", 0), ("in", B, 3), ("in", A, 3), ("in", A, 2), ("slots", 1),
+    ("in", BX, 3), ("ring", 0, 1), ("ring", 1, 0), ("in", AX, 2), ("in", C, 0), ("ring", 1, 1), ("ring", 2, 0),
+    ("rest", 1), ("in", DX, 1), ("ring", 2, 1), ("in", X, 3), ("wait_down",), ("cols", A), ("cols", AX),
+    ("in", C, 3), ("ring", 3, 0), ("in", C, 2), ("in", DX, 0), ("in", BX, 2), ("cols", X), ("ring", 3, 1),
+    ("cols", B), ("in", DX, 2), ("cols", C), ("in", DX, 3), ("ring", 4, 0), ("cols", BX), ("ring", 4, 1),
+    ("cols", DX),
 )
 F32 = jnp.float32
 BF16 = jnp.bfloat16
@@ -138,6 +129,22 @@
         kept.append(jnp.where(ids < stor.shape[0], m, jnp.zeros_like(m)))
     bm2[...] = bmt[...].astype(F32).T.astype(BF16)
 
+    loads["acts"].wait()
+    for p in parts:
+        lo, hi = CUTS[p]
+        down = min(hi, COLS) - lo
+        if hi > COLS:
+            for i in range(2):
+                g = jnp.dot(kept[i], og[i * TILE : (i + 1) * TILE], preferred_element_type=F32)
+                g = (adapter_scale * g).astype(BF16)
+                for u in range(8):
+                    gs[p][u, i, :, down:] = g[:, u * UPC : (u + 1) * UPC]
+        for u in range(8):
+            for i in range(2):
+                block = acts[i * TILE : (i + 1) * TILE, u * COLS + lo : u * COLS + lo + down]
+                low = bmt[i * RANK : (i + 1) * RANK, i * TILE : (i + 1) * TILE]
+                gs[p][u, i, :, :down] = jnp.dot(low, block, preferred_element_type=F32).astype(BF16)
+
     pl.semaphore_wait(barrier, len(friends))
 
     seg_copy = pltpu.make_async_remote_copy(
@@ -154,8 +161,10 @@
     }
     sent = []
 
-    def region(piece, chunk, half):
-        return w.at[piece, pl.ds(pl.multiple_of(half * 512 + chunk * CHUNK, CHUNK), CHUNK)]
+    def region(piece, chunk, half, sub=None):
+        rows = CHUNK if sub is None else CHUNK // SUB
+        first = half * 512 + chunk * CHUNK + (0 if sub is None else sub * rows)
+        return w.at[piece, pl.ds(pl.multiple_of(first, rows), rows)]
 
     def push(src, dst, sem, target):
         cp = pltpu.make_async_remote_copy(
@@ -164,9 +173,10 @@
         cp.start()
         sent.append(cp)
 
-    def push_own(chunk, label, target):
-        src = w_h.at[pl.ds(pl.multiple_of(c * 512 + chunk * CHUNK, CHUNK), CHUNK)]
-        push(src, region(t, chunk, c), w_recv.at[label, chunk], target)
+    def push_own(chunk, label, sub, target):
+        rows = CHUNK // SUB
+        src = w_h.at[pl.ds(pl.multiple_of(c * 512 + chunk * CHUNK + sub * rows, rows), rows)]
+        push(src, region(t, chunk, c, sub), w_recv.at[label, chunk, sub], target)
 
     def sib_arrived(label):
         for chunk in range(4):
@@ -176,42 +186,27 @@
     up_y, dn_y, up_x, dn_x, up_z, dn_z = dev(dy=1), dev(dy=-1), dev(dx=1), dev(dx=-1), dev(dz=1), dev(dz=-1)
 
     def own_y(chunk):
-        push_own(chunk, B, up_y)
-        push_own(chunk, A, dn_y)
+        for sub in range(SUB):
+            push_own(chunk, B, sub, up_y)
+            push_own(chunk, A, sub, dn_y)
 
     def own_x():
-        push_own(chunks[0], X, up_x)
-        push_own(chunks[1], X, dn_x)
+        for sub in range(SUB):
+            push_own(chunks[0], X, sub, up_x)
+            push_own(chunks[1], X, sub, dn_x)
 
     g_sent = []
 
     def tiles_out(p):
-        lo, hi = CUTS[p]
-        down = min(hi, COLS) - lo
-        if p == 0:
-            loads["acts"].wait()
-        if hi > COLS:
-            for i in range(2):
-                g = jnp.dot(kept[i], og[i * TILE : (i + 1) * TILE], preferred_element_type=F32)
-                g = (adapter_scale * g).astype(BF16)
-                for u in range(8):
-                    gs[p][u, i, :, down:] = g[:, u * UPC : (u + 1) * UPC]
-        for n, (dy, dx, flip) in enumerate(order):
-            u = tensor_of(dy, dx)
-            if n % 2 == 0:
-                for i in range(2):
-                    block = acts[i * TILE : (i + 1) * TILE, pl.ds(pl.multiple_of(u * COLS + lo, 128), down)]
-                    low = bmt[i * RANK : (i + 1) * RANK, i * TILE : (i + 1) * TILE]
-                    gs[p][u, i, :, :down] = jnp.dot(low, block, preferred_element_type=F32).astype(BF16)
-            if n == len(order) - 1:
-                gr[p][0, t] = gs[p][t]
-            else:
-                cp = pltpu.make_async_remote_copy(
-                    src_ref=gs[p].at[u], dst_ref=gr[p].at[flip, t], send_sem=g_send.at[p, n], recv_sem=g_recv.at[p, n],
-                    device_id=peer(dy, dx, flip), device_id_type=MESH,
-                )
-                cp.start()
-                g_sent.append(cp)
+        for n, (dy, dx, flip) in enumerate(order[:-1]):
+            cp = pltpu.make_async_remote_copy(
+                src_ref=gs[p].at[tensor_of(dy, dx)], dst_ref=gr[p].at[flip, t],
+                send_sem=g_send.at[p, n], recv_sem=g_recv.at[p, n],
+                device_id=peer(dy, dx, flip), device_id_type=MESH,
+            )
+            cp.start()
+            g_sent.append(cp)
+        gr[p][0, t] = gs[p][t]
 
     def wait_tiles(p):
         for dy, dx, flip in order[:-1]:
@@ -383,10 +378,12 @@
     }
 
     def chunk_in(label, n):
+        for sub in range(SUB):
+            place = region(where[label], chunks[n], c, sub)
+            pltpu.make_async_copy(place, place, w_recv.at[label, chunks[n], sub]).wait()
+            for new, target in passing.get((label, n), ()):
+                push(place, place, w_recv.at[new, chunks[n], sub], target)
         place = region(where[label], chunks[n], c)
-        pltpu.make_async_copy(place, place, w_recv.at[label, chunks[n]]).wait()
-        for new, target in passing.get((label, n), ()):
-            push(place, place, w_recv.at[new, chunks[n]], target)
         push(place, place, sib_recv.at[label, chunks[n]], dev(dc=1))
 
     def columns(label):
@@ -502,8 +499,8 @@
             pltpu.SMEM((128,), jnp.int32),
             dma((5,)),
             dma((8,)),
-            dma((64,)),
-            dma((7, 4)),
+            dma((28 * (SUB + 1),)),
+            dma((7, 4, SUB)),
             dma((7, 4)),
             dma((7,)),
             dma((7,)),

time: 84.7 us -> 75.1 us (0.89)
  Pallas kernels: 83.9 us -> 74.3 us
    pallas_call x1, Pallas kernels: 79.8 us -> 70.2 us  [body(): pl.pallas_call(kernel, out_shape=(jax.ShapeDtypeStruct((ROWS, WIDTH), BF1...]
where the time goes in v3:
time: 75.1 us; the launch traced here: 75 us
  Pallas kernels  74.3 us (99%)
    pallas_call x1, Pallas kernels, body(): pl.pallas_call(kernel, out_shape=(jax.ShapeDtypeStruct((ROWS, WIDTH), BF1...  70.2 us
    pallas_call x1, Pallas kernels, body(): pl.pallas_call(finish, out_shape=(jax.ShapeDtypeStruct((ROWS, WIDTH), BF1...  4.16 us

profile of v3, /device:TPU:1, one launch (start us, length us, event | category | flops | bytes accessed | tf_op | source)
XLA Modules:
  0.0 75.0 jit_solution(6577626294295382264)
XLA Ops:
  0.6 70.2 %fused.1 = (bf16[256,8192]{1,0:T(8,128)(2,1)}, f32[4,16,1024]{2,1,0:T(8,128)}, f32[4,16,128]{2,1,0:T(8,128)}) custom-call(bf16[256,8192]{1,0:T(8,128)(2,1)} %acts_h.1, bf16[256,1024]{1,0:T(8,128)(2,1)} %og_h.1, bf16[16,256]{1,0:T(8,128)(2,1)} %bitcast.7, s32[1,256]{1,0:T(1,128)} %bitcast.9, s32[1,13]{1,0:T(1,128)} %seg.1, s32[13,32]{1,0:T(8,128)} %bitcast.8, ...), custom_call_target="tpu_custom_call" | custom-call | flops 4294967296 | bytes 12582912 | tf_op jit(solution)/shard_map/fused/pallas_call | solution.py:468
  70.8 4.2 %finish.1 = (bf16[256,8192]{1,0:T(8,128)(2,1)}, f32[4,16,1024]{2,1,0:T(8,128)}, f32[4,16,1024]{2,1,0:T(8,128)}, f32[4,16,1024]{2,1,0:T(8,128)}, f32[4,16,128]{2,...) custom-call(bf16[256,8192]{1,0:T(8,128)(2,1)} %get-tuple-element.10.tmp, ...), custom_call_target="tpu_custom_call" | custom-call | tf_op jit(solution)/shard_map/finish/pallas_call | solution.py:524

commit v4 on v3

--- a/solution.py
+++ b/solution.py
@@ -31,7 +31,7 @@
 CUTS = ((0, 640), (640, PAY))
 BLOCK = 256
 SUB = 2
-VMEM_LIMIT = 56 << 20
+VMEM_LIMIT = 58 << 20
 SEQ = (
     ("own_y", 0), ("own_y", 1), ("own_x",), ("tables",), ("in", B, 0), ("in", A, 0), ("in", B, 1), ("in", A, 1),
     ("tiles", 0), ("tiles", 1), ("in", X, 0), ("in", AX, 1), ("in", BX, 1), ("in", X, 1), ("in", AX, 0),
@@ -58,11 +58,11 @@
 
 def kernel(
     acts_h, og_h, midt, rid, seg, apst, stor, w_h, sd_h, su_h,
-    out_h, gd, gu,
+    out, gd, gu,
     acts, og, sd, su, w, xd, dn,
     gs0, gs1, gr0, gr1, sl0, sl1, dns0, dns1, us0, us1, ur0, ur1, ds0, ds1, dr0, dr1,
-    bmt, bm2, ost, tslot, seg2, sr, tab,
-    in_sem, out_sem, w_send, w_recv, sib_recv, dn_send, dn_recv, g_send, g_recv,
+    bmt, bm2, tslot, seg2, sr, tab,
+    in_sem, w_send, w_recv, sib_recv, dn_send, dn_recv, g_send, g_recv,
     s_send, s_recv, r_send, r_recv, m_sem,
 ):
     gs, gr, sl, dns = (gs0, gs1), (gr0, gr1), (sl0, sl1), (dns0, dns1)
@@ -240,19 +240,13 @@
             place = dn.at[tensor_of(dy, dx)]
             pltpu.make_async_copy(place, place, dn_recv.at[plane.index(((4 - dy) % 4, dx))]).wait()
 
-    outs = []
-
     def in_grad(piece):
         for j in range(COLS // BLOCK):
             rows = pl.ds(j * BLOCK, BLOCK)
             cols = pl.ds(pl.multiple_of(piece * COLS + j * BLOCK, BLOCK), BLOCK)
             full = lax.dot_general(og[...], w[piece, rows], (((1,), (1,)), ((), ())), preferred_element_type=F32)
             low = jnp.dot(bm2[...], dn[piece, :, rows], preferred_element_type=F32)
-            ost[:, cols] = (full + low).astype(BF16)
-        cols = pl.ds(pl.multiple_of(piece * COLS, COLS), COLS)
-        cp = pltpu.make_async_copy(ost.at[:, cols], out_h.at[:, cols], out_sem.at[len(outs)])
-        cp.start()
-        outs.append(cp)
+            out[:, cols] = (full + low).astype(BF16)
 
     def find(n, _):
         q, rest = n // 32, n % 32
@@ -412,39 +406,33 @@
 
     for cp in sent + g_sent + dn_sent + s_sent + r_sent:
         cp.wait_send()
-    for cp in outs:
-        cp.wait()
-
-
-def finish(tmp, *refs):
-    ins, outs, bufs, stage, sems = refs[:8], refs[8:15], refs[15:29], refs[29], refs[30]
-    step = ROWS // 8
-    loads = [pltpu.make_async_copy(ins[i], bufs[i], sems.at[i]) for i in range(8)]
-    for i in range(8):
-        rows = pl.ds(i * step, step)
-        loads.append(pltpu.make_async_copy(tmp.at[rows], stage.at[rows], sems.at[8 + i]))
+
+
+def finish(tmp, grad_down, *refs):
+    states, grad_up, outs, bufs, sems = refs[:3], refs[3], refs[7:14], refs[14:26], refs[26]
+    states += refs[4:7]
+    loads = [pltpu.make_async_copy(states[i], bufs[i], sems.at[i]) for i in range(6)]
     for cp in loads:
         cp.start()
     moves = []
 
     def leave(src, dst):
-        cp = pltpu.make_async_copy(src, dst, sems.at[16 + len(moves)])
+        cp = pltpu.make_async_copy(src, dst, sems.at[6 + len(moves)])
         cp.start()
         moves.append(cp)
 
-    for cp in loads[:8]:
+    step = ROWS // 8
+    for i in range(8):
+        rows = pl.ds(i * step, step)
+        leave(tmp.at[rows], outs[0].at[rows])
+    for cp in loads:
         cp.wait()
-    for half in range(2):
-        gr, pr, fi, se = bufs[half * 4 : half * 4 + 4]
-        new = adam_update(pr[...], fi[...], se[...], gr[...])
+    for half, grad in enumerate((grad_down, grad_up)):
+        new = adam_update(*(ref[...] for ref in bufs[half * 3 : half * 3 + 3]), grad[...])
         for i in range(3):
             n = half * 3 + i
-            bufs[8 + n][...] = new[i]
-            leave(bufs[8 + n], outs[1 + n])
-        for i in range(half * 4, half * 4 + 4):
-            rows = pl.ds(i * step, step)
-            loads[8 + i].wait()
-            leave(stage.at[rows], outs[0].at[rows])
+            bufs[6 + n][...] = new[i]
+            leave(bufs[6 + n], outs[1 + n])
     for cp in moves:
         cp.wait()
 
@@ -468,12 +456,12 @@
     tmp, grad_down, grad_up = pl.pallas_call(
         kernel,
         out_shape=(
-            jax.ShapeDtypeStruct((ROWS, WIDTH), BF16),
-            jax.ShapeDtypeStruct(down_shape, F32),
-            jax.ShapeDtypeStruct(up_shape, F32),
+            pltpu.VMEM((ROWS, WIDTH), BF16),
+            pltpu.VMEM(down_shape, F32),
+            pltpu.VMEM(up_shape, F32),
         ),
         in_specs=[hbm, hbm, vmem, vmem, smem, smem, smem, hbm, hbm, hbm],
-        out_specs=(hbm, vmem, vmem),
+        out_specs=(vmem, vmem, vmem),
         scratch_shapes=[
             pltpu.VMEM((ROWS, WIDTH), BF16),
             pltpu.VMEM((ROWS, KVW), BF16),
@@ -492,13 +480,11 @@
             *each((4, STORED, RANK), BF16),
             pltpu.VMEM((2 * RANK, ROWS), BF16),
             pltpu.VMEM((ROWS, 2 * RANK), BF16),
-            pltpu.VMEM((ROWS, WIDTH), BF16),
             pltpu.SMEM((TILES,), jnp.int32),
             pltpu.SMEM((1, SLOTS), jnp.int32),
             pltpu.SMEM((4 * SLOTS,), jnp.int32),
             pltpu.SMEM((128,), jnp.int32),
             dma((5,)),
-            dma((8,)),
             dma((28 * (SUB + 1),)),
             dma((7, 4, SUB)),
             dma((7, 4)),
@@ -524,13 +510,9 @@
     return pl.pallas_call(
         finish,
         out_shape=(jax.ShapeDtypeStruct((ROWS, WIDTH), BF16), *state_down, *state_up),
-        in_specs=[hbm] * 9,
+        in_specs=[vmem, vmem, hbm, hbm, hbm, vmem, hbm, hbm, hbm],
         out_specs=(hbm,) * 7,
-        scratch_shapes=[pltpu.VMEM(down_shape, F32)] * 4
-        + [pltpu.VMEM(up_shape, F32)] * 4
-        + [pltpu.VMEM(down_shape, F32)] * 3
-        + [pltpu.VMEM(up_shape, F32)] * 3
-        + [pltpu.VMEM((ROWS, WIDTH), BF16), dma((30,))],
+        scratch_shapes=([pltpu.VMEM(down_shape, F32)] * 3 + [pltpu.VMEM(up_shape, F32)] * 3) * 2 + [dma((20,))],
         name="finish",
     )(
         tmp, grad_down, down_matrix_rows, down_first_moment, down_second_moment,

time: 75.1 us -> 78 us (1.039)
  local copies, waits for them, and re-layouts: 0 us -> 3.23 us
    unnamed x0 -> x6, local copies, waits for them, and re-layouts: none -> 3.23 us
    pallas_call x1, Pallas kernels: 70.2 us -> 68.8 us  [body(): pl.pallas_call(kernel, out_shape=(pltpu.VMEM((ROWS, WIDTH), BF16), pltpu....]
    pallas_call x1, Pallas kernels: 4.16 us -> 5.21 us  [body(): pl.pallas_call(finish, out_shape=(jax.ShapeDtypeStruct((ROWS, WIDTH), BF1...]
where the time goes in v4:
time: 78 us; the launch traced here: 77.9 us
  Pallas kernels  74 us (95%)
  local copies, waits for them, and re-layouts  3.23 us (4%)
    pallas_call x1, Pallas kernels, body(): pl.pallas_call(kernel, out_shape=(pltpu.VMEM((ROWS, WIDTH), BF16), pltpu....  68.8 us
    pallas_call x1, Pallas kernels, body(): pl.pallas_call(finish, out_shape=(jax.ShapeDtypeStruct((ROWS, WIDTH), BF1...  5.21 us
    unnamed x6, local copies, waits for them, and re-layouts  3.23 us

profile of v4, /device:TPU:1, one launch (start us, length us, event | category | flops | bytes accessed | tf_op | source)
XLA Modules:
  0.0 77.9 jit_solution(6087819014348826332)
XLA Ops:
  0.6 68.8 %fused.1 = (bf16[256,8192]{1,0:T(8,128)(2,1)S(1)}, f32[4,16,1024]{2,1,0:T(8,128)S(1)}, f32[4,16,128]{2,1,0:T(8,128)S(1)}) custom-call(bf16[256,8192]{1,0:T(8,128)(2,1)} %acts_h.1, bf16[256,1024]{1,0:T(8,128)(2,1)} %og_h.1, bf16[16,256]{1,0:T(8,128)(2,1)} %bitcast.7, s32[1,256]{1,0:T(1,128)} %bitcast.9, s32[1,13]{1,0:T(1,128)} %seg.1, s32[13,32]{1,0:T(8,128)} %bitcast.8, ...), custom_call_target="tpu_custom_call" | custom-call | flops 4294967296 | bytes 12582912 | tf_op jit(solution)/shard_map/fused/pallas_call | solution.py:456
  69.4 0.0 copy-start
  69.4 1.9 %copy-done = bf16[256,8192]{1,0:T(8,128)(2,1)} copy-done((bf16[256,8192]{1,0:T(8,128)(2,1)}, bf16[256,8192]{1,0:T(8,128)(2,1)S(1)}, u32[]{:S(2)}) %copy-start) | copy-done | bytes 4194328
  71.4 0.0 copy-start.1
  71.4 0.7 copy-done.1
  72.1 0.0 copy-start.2
  72.1 0.6 copy-done.2
  72.7 5.2 %finish.1 = (bf16[256,8192]{1,0:T(8,128)(2,1)}, f32[4,16,1024]{2,1,0:T(8,128)}, f32[4,16,1024]{2,1,0:T(8,128)}, f32[4,16,1024]{2,1,0:T(8,128)}, f32[4,16,128]{2,...) custom-call(bf16[256,8192]{1,0:T(8,128)(2,1)} %copy-done, f32[4,16,1024]{2,1,0:T(8,128)} %copy-done.1, ...), custom_call_target="tpu_custom_call" | custom-call | tf_op jit(solution)/shard_map/finish/pallas_call | solution.py:510
Async XLA Ops:
  69.4 1.9 %copy-start = (bf16[256,8192]{1,0:T(8,128)(2,1)}, bf16[256,8192]{1,0:T(8,128)(2,1)S(1)}, u32[]{:S(2)}) copy-start(bf16[256,8192]{1,0:T(8,128)(2,1)S(1)} %get-tuple-element.10.tmp) | copy-start | bytes 12582916
  71.4 0.7 copy-start.1
  72.1 0.6 copy-start.2

commit v5 on v4

--- a/solution.py
+++ b/solution.py
@@ -33,15 +33,15 @@
 SUB = 2
 VMEM_LIMIT = 58 << 20
 SEQ = (
-    ("own_y", 0), ("own_y", 1), ("own_x",), ("tables",), ("in", B, 0), ("in", A, 0), ("in", B, 1), ("in", A, 1),
-    ("tiles", 0), ("tiles", 1), ("in", X, 0), ("in", AX, 1), ("in", BX, 1), ("in", X, 1), ("in", AX, 0),
-    ("in", X, 2), ("in", B, 2), ("downs",), ("cols", None), ("in", BX, 0), ("in", C, 1), ("in", AX, 3),
-    ("slots", 0), ("ring", 0, 0), ("rest", 0), ("in", B, 3), ("in", A, 3), ("in", A, 2), ("slots", 1),
-    ("in", BX, 3), ("ring", 0, 1), ("ring", 1, 0), ("in", AX, 2), ("in", C, 0), ("ring", 1, 1), ("ring", 2, 0),
-    ("rest", 1), ("in", DX, 1), ("ring", 2, 1), ("in", X, 3), ("wait_down",), ("cols", A), ("cols", AX),
-    ("in", C, 3), ("ring", 3, 0), ("in", C, 2), ("in", DX, 0), ("in", BX, 2), ("cols", X), ("ring", 3, 1),
-    ("cols", B), ("in", DX, 2), ("cols", C), ("in", DX, 3), ("ring", 4, 0), ("cols", BX), ("ring", 4, 1),
-    ("cols", DX),
+    ("own_y", 0), ("own_x",), ("local",), ("own_y", 1), ("tiles", 0), ("in", X, 1), ("in", A, 0), ("in", X, 0),
+    ("in", B, 0), ("in", A, 1), ("in", B, 1), ("tables",), ("in", BX, 0), ("slots", 0), ("tiles", 1),
+    ("in", BX, 1), ("in", AX, 1), ("ring", 0, 0), ("in", AX, 0), ("downs",), ("in", B, 2), ("in", X, 2),
+    ("in", C, 0), ("slots", 1), ("ring", 0, 1), ("in", A, 3), ("in", A, 2), ("in", B, 3), ("ring", 1, 0),
+    ("rest", 1), ("in", C, 1), ("cols", None), ("in", BX, 3), ("ring", 1, 1), ("wait_down",), ("in", X, 3),
+    ("in", AX, 2), ("rest", 0), ("in", BX, 2), ("ring", 2, 0), ("in", C, 2), ("cols", X), ("ring", 2, 1),
+    ("in", AX, 3), ("cols", BX), ("ring", 3, 0), ("cols", AX), ("in", DX, 0), ("ring", 3, 1), ("in", C, 3),
+    ("cols", A), ("in", DX, 1), ("in", DX, 2), ("cols", B), ("in", DX, 3), ("ring", 4, 0), ("cols", C),
+    ("ring", 4, 1), ("cols", DX),
 )
 F32 = jnp.float32
 BF16 = jnp.bfloat16
@@ -113,38 +113,6 @@
 
     lax.fori_loop(0, TILES, tile_slot, 0)
 
-    loads["og"].wait()
-    loads["su"].wait()
-    kept = []
-    bmt[...] = jnp.zeros_like(bmt)
-    for i in range(2):
-        slot = tslot[2 * t + i]
-        ids = rid[:, i * TILE : (i + 1) * TILE]
-        prod = lax.dot_general(
-            su[slot], og[i * TILE : (i + 1) * TILE], (((1,), (1,)), ((), ())), preferred_element_type=F32
-        )
-        own = jnp.where(ids == apst[slot, a], adapter_scale * prod, 0.0)
-        bmt[i * RANK : (i + 1) * RANK, i * TILE : (i + 1) * TILE] = own.astype(BF16)
-        m = midt[:, i * TILE : (i + 1) * TILE]
-        kept.append(jnp.where(ids < stor.shape[0], m, jnp.zeros_like(m)))
-    bm2[...] = bmt[...].astype(F32).T.astype(BF16)
-
-    loads["acts"].wait()
-    for p in parts:
-        lo, hi = CUTS[p]
-        down = min(hi, COLS) - lo
-        if hi > COLS:
-            for i in range(2):
-                g = jnp.dot(kept[i], og[i * TILE : (i + 1) * TILE], preferred_element_type=F32)
-                g = (adapter_scale * g).astype(BF16)
-                for u in range(8):
-                    gs[p][u, i, :, down:] = g[:, u * UPC : (u + 1) * UPC]
-        for u in range(8):
-            for i in range(2):
-                block = acts[i * TILE : (i + 1) * TILE, u * COLS + lo : u * COLS + lo + down]
-                low = bmt[i * RANK : (i + 1) * RANK, i * TILE : (i + 1) * TILE]
-                gs[p][u, i, :, :down] = jnp.dot(low, block, preferred_element_type=F32).astype(BF16)
-
     pl.semaphore_wait(barrier, len(friends))
 
     seg_copy = pltpu.make_async_remote_copy(
@@ -194,6 +162,39 @@
         for sub in range(SUB):
             push_own(chunks[0], X, sub, up_x)
             push_own(chunks[1], X, sub, dn_x)
+
+    def local():
+        loads["og"].wait()
+        loads["su"].wait()
+        kept = []
+        bmt[...] = jnp.zeros_like(bmt)
+        for i in range(2):
+            slot = tslot[2 * t + i]
+            ids = rid[:, i * TILE : (i + 1) * TILE]
+            prod = lax.dot_general(
+                su[slot], og[i * TILE : (i + 1) * TILE], (((1,), (1,)), ((), ())), preferred_element_type=F32
+            )
+            own = jnp.where(ids == apst[slot, a], adapter_scale * prod, 0.0)
+            bmt[i * RANK : (i + 1) * RANK, i * TILE : (i + 1) * TILE] = own.astype(BF16)
+            m = midt[:, i * TILE : (i + 1) * TILE]
+            kept.append(jnp.where(ids < stor.shape[0], m, jnp.zeros_like(m)))
+        bm2[...] = bmt[...].astype(F32).T.astype(BF16)
+
+        loads["acts"].wait()
+        for p in parts:
+            lo, hi = CUTS[p]
+            down = min(hi, COLS) - lo
+            if hi > COLS:
+                for i in range(2):
+                    g = jnp.dot(kept[i], og[i * TILE : (i + 1) * TILE], preferred_element_type=F32)
+                    g = (adapter_scale * g).astype(BF16)
+                    for u in range(8):
+                        gs[p][u, i, :, down:] = g[:, u * UPC : (u + 1) * UPC]
+            for u in range(8):
+                for i in range(2):
+                    block = acts[i * TILE : (i + 1) * TILE, u * COLS + lo : u * COLS + lo + down]
+                    low = bmt[i * RANK : (i + 1) * RANK, i * TILE : (i + 1) * TILE]
+                    gs[p][u, i, :, :down] = jnp.dot(low, block, preferred_element_type=F32).astype(BF16)
 
     g_sent = []
 
@@ -389,6 +390,7 @@
             in_grad(where[label])
 
     steps = {
+        "local": local,
         "own_y": lambda n: own_y(chunks[n]),
         "own_x": own_x,
         "tiles": tiles_out,
@@ -513,6 +515,7 @@
         in_specs=[vmem, vmem, hbm, hbm, hbm, vmem, hbm, hbm, hbm],
         out_specs=(hbm,) * 7,
         scratch_shapes=([pltpu.VMEM(down_shape, F32)] * 3 + [pltpu.VMEM(up_shape, F32)] * 3) * 2 + [dma((20,))],
+        compiler_params=pltpu.CompilerParams(vmem_limit_bytes=8 << 20),
         name="finish",
     )(
         tmp, grad_down, down_matrix_rows, down_first_moment, down_second_moment,

time: 78 us -> 72.6 us (0.931)
  local copies, waits for them, and re-layouts: 3.23 us -> 0.03 us
  Pallas kernels: 74 us -> 71.7 us
    unnamed x6 -> x12, local copies, waits for them, and re-layouts: 3.23 us -> 0.03 us
    pallas_call x1, Pallas kernels: 5.21 us -> 2.61 us  [body(): pl.pallas_call(finish, out_shape=(jax.ShapeDtypeStruct((ROWS, WIDTH), BF1...]
where the time goes in v5:
time: 72.6 us; the launch traced here: 72.5 us
  Pallas kernels  71.7 us (99%)
  between operations  0.74 us (1%)
    pallas_call x1, Pallas kernels, body(): pl.pallas_call(kernel, out_shape=(pltpu.VMEM((ROWS, WIDTH), BF16), pltpu....  69.1 us
    pallas_call x1, Pallas kernels, body(): pl.pallas_call(finish, out_shape=(jax.ShapeDtypeStruct((ROWS, WIDTH), BF1...  2.61 us

profile of v5, /device:TPU:1, one launch (start us, length us, event | category | flops | bytes accessed | tf_op | source)
XLA Modules:
  0.0 72.5 jit_solution(16964699849385337133)
XLA Ops:
  0.6 0.0 copy-start
  0.6 0.0 copy-start.1
  0.7 0.0 copy-start.2
  0.7 0.0 copy-start.3
  0.7 0.0 copy-start.4
  0.7 0.0 copy-start.5
  0.7 69.1 %fused.1 = (bf16[256,8192]{1,0:T(8,128)(2,1)S(1)}, f32[4,16,1024]{2,1,0:T(8,128)S(1)}, f32[4,16,128]{2,1,0:T(8,128)S(1)}) custom-call(bf16[256,8192]{1,0:T(8,128)(2,1)} %acts_h.1, bf16[256,1024]{1,0:T(8,128)(2,1)} %og_h.1, bf16[16,256]{1,0:T(8,128)(2,1)} %bitcast.7, s32[1,256]{1,0:T(1,128)} %bitcast.9, s32[1,13]{1,0:T(1,128)} %seg.1, s32[13,32]{1,0:T(8,128)} %bitcast.8, ...), custom_call_target="tpu_custom_call" | custom-call | flops 4294967296 | bytes 12582912 | tf_op jit(solution)/shard_map/fused/pallas_call | solution.py:458
  69.8 0.0 copy-done
  69.8 0.0 copy-done.1
  69.9 0.0 copy-done.2
  69.9 0.0 copy-done.3
  69.9 0.0 copy-done.4
  69.9 0.0 copy-done.5
  69.9 2.6 %finish.1 = (bf16[256,8192]{1,0:T(8,128)(2,1)}, f32[4,16,1024]{2,1,0:T(8,128)}, f32[4,16,1024]{2,1,0:T(8,128)}, f32[4,16,1024]{2,1,0:T(8,128)}, f32[4,16,128]{2,...) custom-call(bf16[256,8192]{1,0:T(8,128)(2,1)S(1)} %get-tuple-element.10.tmp, ...), custom_call_target="tpu_custom_call" | custom-call | tf_op jit(solution)/shard_map/finish/pallas_call | solution.py:512
Async XLA Ops:
  0.6 69.2 %copy-start = (f32[4,16,1024]{2,1,0:T(8,128)S(1)}, f32[4,16,1024]{2,1,0:T(8,128)}, u32[]{:S(2)}) copy-start(f32[4,16,1024]{2,1,0:T(8,128)} %refs_0_.1) | copy-start | bytes 786436
  0.6 69.2 %copy-start.1 = (f32[4,16,1024]{2,1,0:T(8,128)S(1)}, f32[4,16,1024]{2,1,0:T(8,128)}, u32[]{:S(2)}) copy-start(f32[4,16,1024]{2,1,0:T(8,128)} %refs_1_.1) | copy-start | bytes 786436
  0.7 69.2 %copy-start.2 = (f32[4,16,1024]{2,1,0:T(8,128)S(1)}, f32[4,16,1024]{2,1,0:T(8,128)}, u32[]{:S(2)}) copy-start(f32[4,16,1024]{2,1,0:T(8,128)} %refs_2_.1) | copy-start | bytes 786436
  0.7 69.2 %copy-start.3 = (f32[4,16,128]{2,1,0:T(8,128)S(1)}, f32[4,16,128]{2,1,0:T(8,128)}, u32[]{:S(2)}) copy-start(f32[4,16,128]{2,1,0:T(8,128)} %refs_4_.1) | copy-start | bytes 98308
  0.7 69.2 %copy-start.4 = (f32[4,16,128]{2,1,0:T(8,128)S(1)}, f32[4,16,128]{2,1,0:T(8,128)}, u32[]{:S(2)}) copy-start(f32[4,16,128]{2,1,0:T(8,128)} %refs_5_.1) | copy-start | bytes 98308
  0.7 69.2 %copy-start.5 = (f32[4,16,128]{2,1,0:T(8,128)S(1)}, f32[4,16,128]{2,1,0:T(8,128)}, u32[]{:S(2)}) copy-start(f32[4,16,128]{2,1,0:T(8,128)} %refs_6_.1) | copy-start | bytes 98308
